TPU v7x, 32 devices: a whole 2x2x4 slice. The times are simulated.
32 devices in a mesh: ctx: 8 (over z, x), fsdp: 4 (over y, core).
Axes of the slice: x: 2, y: 2, z: 4, core: 2. Of those that a mesh axis runs over, the one named last changes fastest.
Arguments:
- tokens: bfloat16 [4, 4096, 768], P('fsdp', 'ctx'), may hold values from -6 to 6
- positions: int32 [4, 4096], P('fsdp', 'ctx'), may hold values from 0 to 4095, as said below
- documents: int32 [4, 4096], P('fsdp', 'ctx'), may hold values from 0 to 4, as said below
- ln1_gain: bfloat16 [768], P('fsdp'), may hold values from 0.5 to 1.5
- ln1_bias: bfloat16 [768], P('fsdp'), may hold values from -1 to 1
- w_qkv: bfloat16 [768, 2304], P('fsdp'), may hold values from -0.21875 to 0.21875
- bias_qv: bfloat16 [1536], P('fsdp'), may hold values from -1 to 1
- w_out: bfloat16 [768, 768], P('fsdp'), may hold values from -4 to 4
- bias_out: bfloat16 [768], P('fsdp'), may hold values from -1 to 1
- ln2_gain: bfloat16 [768], P('fsdp'), may hold values from 0.5 to 1.5
- ln2_bias: bfloat16 [768], P('fsdp'), may hold values from -1 to 1
- w_fc: bfloat16 [768, 3072], P('fsdp'), may hold values from -0.21875 to 0.21875
- bias_fc: bfloat16 [3072], P('fsdp'), may hold values from -1 to 1
- w_proj: bfloat16 [3072, 768], P('fsdp'), may hold values from -0.109375 to 0.109375
- bias_proj: bfloat16 [768], P('fsdp'), may hold values from -1 to 1
- cotangent: bfloat16 [4, 4096, 768], P('fsdp', 'ctx'), may hold values from -6 to 6
Outputs:
- block_out: bfloat16 [4, 4096, 768], P('fsdp', 'ctx')
- grad_tokens: bfloat16 [4, 4096, 768], P('fsdp', 'ctx')
- grad_ln1_gain: float32 [768], P('fsdp')
- grad_ln1_bias: float32 [768], P('fsdp')
- grad_w_qkv: float32 [768, 2304], P('fsdp')
- grad_bias_qv: float32 [1536], P('fsdp')
- grad_w_out: float32 [768, 768], P('fsdp')
- grad_bias_out: float32 [768], P('fsdp')
- grad_ln2_gain: float32 [768], P('fsdp')
- grad_ln2_bias: float32 [768], P('fsdp')
- grad_w_fc: float32 [768, 3072], P('fsdp')
- grad_bias_fc: float32 [3072], P('fsdp')
- grad_w_proj: float32 [3072, 768], P('fsdp')
- grad_bias_proj: float32 [768], P('fsdp')
Inputs may be any that keep to these rules, and one draw needn't show every extreme that they name: Each device's block of a sequence holds 512 consecutive increasing positions starting at a multiple of 512; the blocks of one sequence hold every position of 0 to 4095 once, in an order that varies from sequence to sequence. `documents`: document numbers never fall as the position rises within a sequence.
All inputs are finite; a program needn't handle non-finite values.
Results may differ from a plain program's by a relative error of at most 0.017.
Values may be sent and summed in bfloat16 or wider, within the bound.
No kernel may reach another device: no remote copies, remote signals or barrier semaphores. Data moves between devices by JAX's collectives and lax.ppermute only.
A program may use at most 192 MiB of HBM per device.

v0:
```python
import jax
import jax.numpy as jnp
from jax import lax
from jax.sharding import PartitionSpec as P

HEADS = 12


EPS = 1e-05
NEG = -1e30


def passed_along(value, axis, by):
    length = lax.axis_size(axis)
    return lax.ppermute(value, axis, [(i, (i + by) % length) for i in range(length)])


def norm_stats(v):
    centered = v - jnp.mean(v, -1, keepdims=True)
    inverse = lax.rsqrt(jnp.mean(centered * centered, -1, keepdims=True) + EPS)
    return (centered * inverse, inverse)


def norm_back(grad_h, normed, inverse, gain):
    grad_normed = grad_h * gain
    return inverse * (
        grad_normed
        - jnp.mean(grad_normed, -1, keepdims=True)
        - normed * jnp.mean(grad_normed * normed, -1, keepdims=True)
    )


def block_mask(query_place, query_doc, key_place, key_doc):
    return (key_place[:, None, :] <= query_place[:, :, None]) & (
        key_doc[:, None, :] == query_doc[:, :, None]
    )


def per_device(
    tokens,
    positions,
    documents,
    ln1_gain,
    ln1_bias,
    w_qkv,
    bias_qv,
    w_out,
    bias_out,
    ln2_gain,
    ln2_bias,
    w_fc,
    bias_fc,
    w_proj,
    bias_proj,
    cotangent,
):
    f32 = jnp.float32
    bf16 = jnp.bfloat16
    seq_count, block_len, model_width = tokens.shape
    n_heads = HEADS
    head_dim = model_width // n_heads
    score_scale = float(head_dim) ** (-0.5)
    cycle_len = lax.axis_size("ctx")
    my_index = lax.axis_index("ctx")
    shape_heads = (seq_count, block_len, n_heads, head_dim)
    all_places, all_docs = (
        lax.all_gather(positions, "ctx", axis=1, tiled=True),
        lax.all_gather(documents, "ctx", axis=1, tiled=True),
    )

    def source_ids(step):
        source = (my_index - step) % cycle_len
        return (
            lax.dynamic_slice_in_dim(all_places, source * block_len, block_len, 1),
            lax.dynamic_slice_in_dim(all_docs, source * block_len, block_len, 1),
        )

    g_one, b_one, wqkv_all, bqv_all, wout_all, bout_all = (
        lax.all_gather(ln1_gain, "fsdp", axis=0, tiled=True),
        lax.all_gather(ln1_bias, "fsdp", axis=0, tiled=True),
        lax.all_gather(w_qkv, "fsdp", axis=0, tiled=True),
        lax.all_gather(bias_qv, "fsdp", axis=0, tiled=True),
        lax.all_gather(w_out, "fsdp", axis=0, tiled=True),
        lax.all_gather(bias_out, "fsdp", axis=0, tiled=True),
    )
    gain_one = g_one.astype(f32)
    x = tokens.astype(f32).reshape(-1, model_width)
    normed_one, inverse_one = norm_stats(x)
    h_one = (normed_one * gain_one + b_one.astype(f32)).astype(bf16)
    bias_all = jnp.concatenate(
        [
            bqv_all[:model_width].astype(f32),
            jnp.zeros((model_width,), f32),
            bqv_all[model_width:].astype(f32),
        ]
    )
    qkv = jnp.dot(h_one, wqkv_all, preferred_element_type=f32) + bias_all
    q = qkv[:, :model_width].astype(bf16).reshape(shape_heads)
    k = qkv[:, model_width : 2 * model_width].astype(bf16).reshape(shape_heads)
    v = qkv[:, 2 * model_width :].astype(bf16).reshape(shape_heads)

    def scores(query_rows, key_rows):
        return (
            jnp.einsum("sqhc,skhc->shqk", query_rows, key_rows, preferred_element_type=f32)
            * score_scale
        )

    def probs(s, visible, log_total):
        return jnp.where(visible, jnp.exp(s - log_total[..., None]), 0.0)

    stat_shape = (seq_count, n_heads, block_len)

    def online_step(step, carry):
        key_rows, value_rows, row_max, row_sum, summed = carry
        key_place, key_doc = source_ids(step)
        visible = block_mask(positions, documents, key_place, key_doc)[:, None]

        def online_work(row_max, row_sum, summed):
            s = jnp.where(visible, scores(q, key_rows), NEG)
            new_max = jnp.maximum(row_max, jnp.max(s, -1))
            factor = jnp.exp(row_max - new_max)
            weights_raw = jnp.where(visible, jnp.exp(s - new_max[..., None]), 0.0)
            new_sum = row_sum * factor + jnp.sum(weights_raw, -1)
            added = jnp.einsum(
                "shqk,skhc->sqhc", weights_raw.astype(bf16), value_rows, preferred_element_type=f32
            )
            return (new_max, new_sum, summed * jnp.swapaxes(factor, 1, 2)[..., None] + added)

        row_max, row_sum, summed = lax.cond(
            jnp.any(visible), online_work, lambda a, b, c: (a, b, c), row_max, row_sum, summed
        )
        return (key_rows, value_rows, row_max, row_sum, summed)

    def online_loop(step, carry):
        key_rows, value_rows = passed_along((carry[0], carry[1]), "ctx", 1)
        return online_step(step, (key_rows, value_rows, carry[2], carry[3], carry[4]))

    first = online_step(
        0,
        (
            k,
            v,
            jnp.full(stat_shape, NEG, f32),
            jnp.zeros(stat_shape, f32),
            jnp.zeros(shape_heads, f32),
        ),
    )
    _, _, row_max, row_sum, summed = lax.fori_loop(1, cycle_len, online_loop, first)
    log_total = row_max + jnp.log(row_sum)
    attended = summed / jnp.swapaxes(row_sum, 1, 2)[..., None]
    attended_low = attended.reshape(-1, model_width).astype(bf16)
    x_two = x + jnp.dot(attended_low, wout_all, preferred_element_type=f32) + bout_all.astype(f32)
    g_two, b_two, wfc_all, bfc_all, wproj_all, bproj_all = (
        lax.all_gather(ln2_gain, "fsdp", axis=0, tiled=True),
        lax.all_gather(ln2_bias, "fsdp", axis=0, tiled=True),
        lax.all_gather(w_fc, "fsdp", axis=0, tiled=True),
        lax.all_gather(bias_fc, "fsdp", axis=0, tiled=True),
        lax.all_gather(w_proj, "fsdp", axis=0, tiled=True),
        lax.all_gather(bias_proj, "fsdp", axis=0, tiled=True),
    )
    gain_two = g_two.astype(f32)
    normed_two, inverse_two = norm_stats(x_two)
    h_two = (normed_two * gain_two + b_two.astype(f32)).astype(bf16)
    pre_act = jnp.dot(h_two, wfc_all, preferred_element_type=f32) + bfc_all.astype(f32)
    activated, gelu_pull = jax.vjp(lambda t: jax.nn.gelu(t, approximate=True), pre_act)
    activated_low = activated.astype(bf16)
    result = (
        x_two
        + jnp.dot(activated_low, wproj_all, preferred_element_type=f32)
        + bproj_all.astype(f32)
    )
    block_out = result.astype(bf16).reshape(tokens.shape)
    cot_rows = cotangent.reshape(-1, model_width)
    grad_y = cot_rows.astype(f32)
    grad_bproj = jnp.sum(grad_y, 0)
    grad_wproj = jnp.einsum("tf,td->fd", activated_low, cot_rows, preferred_element_type=f32)
    grad_act = jnp.einsum("td,fd->tf", cot_rows, wproj_all, preferred_element_type=f32)
    grad_pre = gelu_pull(grad_act)[0].astype(bf16)
    grad_bfc = jnp.sum(grad_pre.astype(f32), 0)
    grad_wfc = jnp.einsum("td,tf->df", h_two, grad_pre, preferred_element_type=f32)
    grad_h_two = jnp.einsum("tf,df->td", grad_pre, wfc_all, preferred_element_type=f32)
    grad_g_two = jnp.sum(grad_h_two * normed_two, 0)
    grad_b_two = jnp.sum(grad_h_two, 0)
    grad_x_two = grad_y + norm_back(grad_h_two, normed_two, inverse_two, gain_two)
    grad_branch = grad_x_two.astype(bf16)
    grad_bout = jnp.sum(grad_branch.astype(f32), 0)
    grad_wout = jnp.einsum("td,te->de", attended_low, grad_branch, preferred_element_type=f32)
    grad_att = jnp.einsum("te,de->td", grad_branch, wout_all, preferred_element_type=f32)
    grad_att_low = grad_att.astype(bf16).reshape(shape_heads)
    delta = jnp.swapaxes(jnp.sum(grad_att_low.astype(f32) * attended, -1), 1, 2)

    def grad_block(query_rows, grad_rows, log_rows, delta_rows, key_rows, value_rows, visible):
        prob = probs(scores(query_rows, key_rows), visible, log_rows)
        grad_value = jnp.einsum(
            "shqk,sqhc->skhc", prob.astype(bf16), grad_rows, preferred_element_type=f32
        )
        grad_prob = jnp.einsum("sqhc,skhc->shqk", grad_rows, value_rows, preferred_element_type=f32)
        grad_score = (prob * (grad_prob - delta_rows[..., None])).astype(bf16)
        grad_query = (
            jnp.einsum("shqk,skhc->sqhc", grad_score, key_rows, preferred_element_type=f32)
            * score_scale
        )
        grad_key = (
            jnp.einsum("shqk,sqhc->skhc", grad_score, query_rows, preferred_element_type=f32)
            * score_scale
        )
        return (grad_query, grad_key, grad_value)

    zero_heads = jnp.zeros(shape_heads, f32)

    def key_step(step, carry):
        key_rows, value_rows, grad_q, grad_k, grad_v = carry
        key_place, key_doc = source_ids(step)
        visible = block_mask(positions, documents, key_place, key_doc)[:, None]

        def key_work(grad_q, grad_k, grad_v):
            part_q, part_k, part_v = grad_block(
                q, grad_att_low, log_total, delta, key_rows, value_rows, visible
            )
            return (grad_q + part_q, grad_k + part_k, grad_v + part_v)

        grad_q, grad_k, grad_v = lax.cond(
            jnp.any(visible), key_work, lambda a, b, c: (a, b, c), grad_q, grad_k, grad_v
        )
        return (key_rows, value_rows, grad_q, grad_k, grad_v)

    def pass_key_grads(grad_k, grad_v):
        return (
            passed_along(grad_k.astype(jnp.bfloat16), "ctx", 1).astype(grad_k.dtype),
            passed_along(grad_v.astype(jnp.bfloat16), "ctx", 1).astype(grad_v.dtype),
        )

    def key_loop(step, carry):
        key_rows, value_rows, grad_q, grad_k, grad_v = key_step(step - 1, carry)
        grad_k, grad_v = pass_key_grads(grad_k, grad_v)
        key_rows, value_rows = passed_along((key_rows, value_rows), "ctx", 1)
        return (key_rows, value_rows, grad_q, grad_k, grad_v)

    carried = lax.fori_loop(1, cycle_len, key_loop, (k, v, zero_heads, zero_heads, zero_heads))
    _, _, grad_q, grad_k, grad_v = key_step(cycle_len - 1, carried)
    grad_k, grad_v = pass_key_grads(grad_k, grad_v)
    grad_q_low = grad_q.reshape(-1, model_width).astype(bf16)
    grad_k_low = grad_k.reshape(-1, model_width).astype(bf16)
    grad_v_low = grad_v.reshape(-1, model_width).astype(bf16)
    grad_qkv = jnp.concatenate([grad_q_low, grad_k_low, grad_v_low], -1)
    grad_bqv = jnp.concatenate(
        [jnp.sum(grad_q_low.astype(f32), 0), jnp.sum(grad_v_low.astype(f32), 0)]
    )
    grad_wqkv = jnp.einsum("td,te->de", h_one, grad_qkv, preferred_element_type=f32)
    grad_h_one = jnp.einsum("te,de->td", grad_qkv, wqkv_all, preferred_element_type=f32)
    grad_g_one = jnp.sum(grad_h_one * normed_one, 0)
    grad_b_one = jnp.sum(grad_h_one, 0)
    grad_x = grad_x_two + norm_back(grad_h_one, normed_one, inverse_one, gain_one)
    grad_tokens = grad_x.astype(bf16).reshape(tokens.shape)
    full_grads = (
        grad_g_one,
        grad_b_one,
        grad_wqkv,
        grad_bqv,
        grad_wout,
        grad_bout,
        grad_g_two,
        grad_b_two,
        grad_wfc,
        grad_bfc,
        grad_wproj,
        grad_bproj,
    )
    owned = (
        ln1_gain,
        ln1_bias,
        w_qkv,
        bias_qv,
        w_out,
        bias_out,
        ln2_gain,
        ln2_bias,
        w_fc,
        bias_fc,
        w_proj,
        bias_proj,
    )
    owners = lax.axis_size("fsdp")
    packed = jnp.concatenate([grad.reshape(owners, -1) for grad in full_grads], 1)
    reduced = (
        lax.psum_scatter(packed.astype(jnp.bfloat16), "fsdp", scatter_dimension=0, tiled=True)
        .astype(jnp.float32)
        .reshape(-1)
    )
    total_len = reduced.shape[0]
    slice_len = -(-total_len // cycle_len)
    spread_rows = reduced.reshape(cycle_len, slice_len)
    mine = lax.psum_scatter(spread_rows, "ctx", scatter_dimension=0, tiled=True)
    reduced = (
        lax.all_gather(mine.astype(jnp.bfloat16), "ctx", axis=0, tiled=True)
        .astype(mine.dtype)
        .reshape(-1)
    )
    pieces = []
    offset = 0
    for shard in owned:
        pieces.append(reduced[offset : offset + shard.size].reshape(shard.shape))
        offset = offset + shard.size
    return (
        block_out,
        grad_tokens,
        pieces[0],
        pieces[1],
        pieces[2],
        pieces[3],
        pieces[4],
        pieces[5],
        pieces[6],
        pieces[7],
        pieces[8],
        pieces[9],
        pieces[10],
        pieces[11],
    )


def solution(mesh):
    return jax.shard_map(
        per_device,
        mesh=mesh,
        in_specs=(
            P("fsdp", "ctx", None),
            P("fsdp", "ctx"),
            P("fsdp", "ctx"),
            P("fsdp"),
            P("fsdp"),
            P("fsdp", None),
            P("fsdp"),
            P("fsdp", None),
            P("fsdp"),
            P("fsdp"),
            P("fsdp"),
            P("fsdp", None),
            P("fsdp"),
            P("fsdp", None),
            P("fsdp"),
            P("fsdp", "ctx", None),
        ),
        out_specs=(
            P("fsdp", "ctx", None),
            P("fsdp", "ctx", None),
            P("fsdp"),
            P("fsdp"),
            P("fsdp", None),
            P("fsdp"),
            P("fsdp", None),
            P("fsdp"),
            P("fsdp"),
            P("fsdp"),
            P("fsdp", None),
            P("fsdp"),
            P("fsdp", None),
            P("fsdp"),
        ),
        check_vma=False,
    )
```

profile of v0, /device:TPU:0, one launch (start us, length us, event | category | flops | bytes accessed | tf_op | source)
XLA Modules:
  0.0 2103.5 jit_solution(10316221890147306831)
XLA Ops:
  38.1 26.3 %all_gather.49 = s32[1,4096]{1,0:T(1,128)S(1)} all-gather(s32[1,512]{1,0:T(1,128)S(1)} %copy-done.30), channel_id=1, replica_groups=mesh['ctx'=8,'fsdp'=4] {'ctx'}, dimensions={1}, use_global_device_ids=true | all-gather | bytes 18432 | tf_op jit(solution)/shard_map/all_gather | solution.py:67
  64.4 26.0 %all_gather.50 = s32[1,4096]{1,0:T(1,128)S(1)} all-gather(s32[1,512]{1,0:T(1,128)S(1)} %copy-done.29), channel_id=1, replica_groups=mesh['ctx'=8,'fsdp'=4] {'ctx'}, dimensions={1}, use_global_device_ids=true | all-gather | bytes 18432 | tf_op jit(solution)/shard_map/all_gather | solution.py:68
  103.5 18.6 conditional.4
  122.2 278.8 %while.49 = (s32[]{:T(128)}, bf16[1,512,12,64]{1,3,2,0:T(8,128)(2,1)}, bf16[1,512,12,64]{1,3,2,0:T(8,128)(2,1)}, f32[1,12,512]{2,1,0:T(8,128)}, f32[1,12,512]{2,...) while((s32[]{:T(128)}, ...), condition=%wide.region_13.14_spmd, body=%wide.region_7.13_spmd.sunk | while | flops 848840704 | bytes 54157868 | solution.py:148
  125.5 18.6 collective-permute-done.1
  170.5 19.3 collective-permute-done.1
  204.9 18.5 collective-permute-done.1
  237.0 18.1 collective-permute-done.1
  255.1 16.7 collective-permute-done
  296.2 16.7 collective-permute-done
  317.6 20.9 collective-permute-done.1
  338.5 16.7 collective-permute-done
  359.8 21.7 %collective-permute-done.1 = bf16[1,512,12,64]{1,3,2,0:T(8,128)(2,1)} collective-permute-done((bf16[1,512,12,64]{1,3,2,0:T(8,128)(2,1)}, bf16[1,512,12,64]{1,3,2,0:T(8,128)(2,1)}, u32[]{:S(2)}, u32[]{:S(2)}) %collective-permute-start.1) | collective-permute-done | bytes 786464 | tf_op jit(solution)/shard_map/while/body/eval_jaxpr/ppermute | solution.py:15
  381.6 16.4 collective-permute-done
  445.9 565.9 %while.50 = (s32[]{:T(128)}, bf16[1,512,12,64]{1,3,2,0:T(8,128)(2,1)S(1)}, bf16[1,512,12,64]{1,3,2,0:T(8,128)(2,1)S(1)}, f32[1,512,12,64]{1,3,2,0:T(8,128)}, f32...) while((s32[]{:T(128)}, ...), condition=%wide.region_24.25_spmd.clone, body=%wide.region_20.0_spmd.clone.sunk | while | flops 2050883584 | bytes 129073960 | solution.py:239
  451.8 17.5 conditional.11
  528.8 15.6 collective-permute-done.3
  549.8 17.5 conditional.11
  570.7 22.5 %collective-permute-done.5 = bf16[1,512,12,64]{1,3,2,0:T(8,128)(2,1)} collective-permute-done((bf16[1,512,12,64]{1,3,2,0:T(8,128)(2,1)}, bf16[1,512,12,64]{1,3,2,0:T(8,128)(2,1)}, u32[]{:S(2)}, u32[]{:S(2)}) %collective-permute-start.5) | collective-permute-done | bytes 786464 | tf_op jit(solution)/shard_map/while/body/eval_jaxpr/ppermute | solution.py:15
  626.8 14.7 collective-permute-done.3
  650.3 22.5 %collective-permute-done.5 = bf16[1,512,12,64]{1,3,2,0:T(8,128)(2,1)} collective-permute-done((bf16[1,512,12,64]{1,3,2,0:T(8,128)(2,1)}, bf16[1,512,12,64]{1,3,2,0:T(8,128)(2,1)}, u32[]{:S(2)}, u32[]{:S(2)}) %collective-permute-start.5) | collective-permute-done | bytes 786464 | tf_op jit(solution)/shard_map/while/body/eval_jaxpr/ppermute | solution.py:15
  729.0 22.5 %collective-permute-done.5 = bf16[1,512,12,64]{1,3,2,0:T(8,128)(2,1)} collective-permute-done((bf16[1,512,12,64]{1,3,2,0:T(8,128)(2,1)}, bf16[1,512,12,64]{1,3,2,0:T(8,128)(2,1)}, u32[]{:S(2)}, u32[]{:S(2)}) %collective-permute-start.5) | collective-permute-done | bytes 786464 | tf_op jit(solution)/shard_map/while/body/eval_jaxpr/ppermute | solution.py:15
  858.8 16.1 collective-permute-done.3
  931.7 16.9 collective-permute-done.3
  996.5 15.3 collective-permute-done.3
  1083.5 45.3 %dynamic-update-slice.14 = bf16[4,1771776]{1,0:T(4,128)(2,1)} dynamic-update-slice(bf16[4,1771776]{1,0:T(4,128)(2,1)} %dynamic-update-slice.13, bf16[4,589824]{1,0:T(4,128)(2,1)} %reshape.754, s32[]{} %constant.319, s32[]{} %constant.328) | dynamic-update-slice | bytes 9437188
  1130.3 45.1 %dynamic-update-slice.16 = bf16[4,1771776]{1,0:T(4,128)(2,1)} dynamic-update-slice(bf16[4,1771776]{1,0:T(4,128)(2,1)} %dynamic-update-slice.15, bf16[4,589824]{1,0:T(4,128)(2,1)} %reshape.756, s32[]{} %constant.319, s32[]{} %constant.330) | dynamic-update-slice | bytes 9437188
  1178.1 332.7 %all-reduce.12.cloned.1.call-done = bf16[4,1771776]{1,0:T(4,128)(2,1)} async-done(((bf16[4,1771776]{1,0:T(4,128)(2,1)}), bf16[4,1771776]{1,0:T(4,128)(2,1)}) %all-reduce.12.cloned.1.call-update) | async-done | bytes 14174224
  1510.7 66.6 %fusion.65 = f32[1771776]{0:T(1024)} fusion(bf16[4,1771776]{1,0:T(4,128)(2,1)} %all-reduce.12.cloned.1.call-done, u32[]{:T(128)} %bitcast.107), kind=kLoop, calls=%fused_computation.91 | loop fusion | flops 1771776 | bytes 10630660 | tf_op jit(solution)/shard_map/reshape;reshape | solution.py:292
  1587.0 279.5 %all-reduce.13 = bf16[8,221472]{1,0:T(8,128)(2,1)} all-reduce(f32[8,221472]{1,0:T(8,128)} %reshape.762), channel_id=3, replica_groups=mesh['ctx'=8,'fsdp'=4] {'ctx'}, use_global_device_ids=true, to_apply=%region_39.40.clone | all-reduce | flops 1771776 | bytes 10630656
  1881.2 95.9 %all-gather.17.cloned.1.call-done = bf16[8,1,221472]{2,1,0:T(2,128)(2,1)} async-done(((bf16[1,1,221472]{2,1,0:T(2,128)(2,1)}), bf16[8,1,221472]{2,1,0:T(2,128)(2,1)}) %all-gather.17.cloned.1.call-update) | async-done | bytes 3543568 | tf_op jit(solution)/shard_map/all_gather | solution.py:295
  1977.1 77.3 %convert_reduce_fusion = f32[8,221472]{1,0:T(8,128)} fusion(bf16[8,1,221472]{2,1,0:T(2,128)(2,1)} %all-gather.17.cloned.1.call-done), kind=kLoop, calls=%fused_computation.89 | loop fusion | flops 1771776 | bytes 10630656 | tf_op jit(solution)/shard_map/convert_element_type | solution.py:296
  (502 shorter events, 766.8 us)
Async XLA Ops:
  7.3 86.4 %all-gather.9.cloned.1.call-start = ((), (), s32[]{:S(2)}) async-start(), calls=%async_computation | async-start | bytes 4423680 | tf_op jit(solution)/shard_map/all_gather | solution.py:81
  8.1 394.6 %all-gather.11.cloned.1.call-start = ((), (), s32[]{:S(2)}) async-start(), calls=%async_computation.1 | async-start | bytes 1474560 | tf_op jit(solution)/shard_map/all_gather | solution.py:83
  8.8 398.7 %all-gather.13.cloned.1.call-start = ((), (), s32[]{:S(2)}) async-start(), calls=%async_computation.2 | async-start | bytes 5898240 | tf_op jit(solution)/shard_map/all_gather | solution.py:156
  9.5 411.6 %all-gather.15.cloned.1.call-start = ((), (), s32[]{:S(2)}) async-start(), calls=%async_computation.3 | async-start | bytes 5898240 | tf_op jit(solution)/shard_map/all_gather | solution.py:158
  10.1 1500.6 %all-reduce.12.cloned.1.call-start = ((), (), s32[]{:S(2)}) async-start(), calls=%async_computation.5 | async-start | bytes 28348416
  168.8 31.5 %collective-permute-start = (bf16[1,512,12,64]{1,3,2,0:T(8,128)(2,1)}, bf16[1,512,12,64]{1,3,2,0:T(8,128)(2,1)S(1)}, u32[]{:S(2)}, u32[]{:S(2)}) collective-permute-start(bf16[1,512,12,64]{1,3,2,0:T(8,128)(2,1)} %get-tuple-element.1458), channel_id=1, source_target_pairs={{0,4},{4,8},{8,12},{12,16},{16,20},{20,24},{24,28},{28,0},{1,5},{5... | collective-permute-start | bytes 2359304 | tf_op jit(solution)/shard_map/while/body/eval_jaxpr/ppermute | solution.py:15
  235.3 36.5 %collective-permute-start = (bf16[1,512,12,64]{1,3,2,0:T(8,128)(2,1)}, bf16[1,512,12,64]{1,3,2,0:T(8,128)(2,1)S(1)}, u32[]{:S(2)}, u32[]{:S(2)}) collective-permute-start(bf16[1,512,12,64]{1,3,2,0:T(8,128)(2,1)} %get-tuple-element.1458), channel_id=1, source_target_pairs={{0,4},{4,8},{8,12},{12,16},{16,20},{20,24},{24,28},{28,0},{1,5},{5... | collective-permute-start | bytes 2359304 | tf_op jit(solution)/shard_map/while/body/eval_jaxpr/ppermute | solution.py:15
  274.7 38.2 %collective-permute-start = (bf16[1,512,12,64]{1,3,2,0:T(8,128)(2,1)}, bf16[1,512,12,64]{1,3,2,0:T(8,128)(2,1)S(1)}, u32[]{:S(2)}, u32[]{:S(2)}) collective-permute-start(bf16[1,512,12,64]{1,3,2,0:T(8,128)(2,1)} %get-tuple-element.1458), channel_id=1, source_target_pairs={{0,4},{4,8},{8,12},{12,16},{16,20},{20,24},{24,28},{28,0},{1,5},{5... | collective-permute-start | bytes 2359304 | tf_op jit(solution)/shard_map/while/body/eval_jaxpr/ppermute | solution.py:15
  315.9 39.3 %collective-permute-start = (bf16[1,512,12,64]{1,3,2,0:T(8,128)(2,1)}, bf16[1,512,12,64]{1,3,2,0:T(8,128)(2,1)S(1)}, u32[]{:S(2)}, u32[]{:S(2)}) collective-permute-start(bf16[1,512,12,64]{1,3,2,0:T(8,128)(2,1)} %get-tuple-element.1458), channel_id=1, source_target_pairs={{0,4},{4,8},{8,12},{12,16},{16,20},{20,24},{24,28},{28,0},{1,5},{5... | collective-permute-start | bytes 2359304 | tf_op jit(solution)/shard_map/while/body/eval_jaxpr/ppermute | solution.py:15
  358.2 39.9 %collective-permute-start = (bf16[1,512,12,64]{1,3,2,0:T(8,128)(2,1)}, bf16[1,512,12,64]{1,3,2,0:T(8,128)(2,1)S(1)}, u32[]{:S(2)}, u32[]{:S(2)}) collective-permute-start(bf16[1,512,12,64]{1,3,2,0:T(8,128)(2,1)} %get-tuple-element.1458), channel_id=1, source_target_pairs={{0,4},{4,8},{8,12},{12,16},{16,20},{20,24},{24,28},{28,0},{1,5},{5... | collective-permute-start | bytes 2359304 | tf_op jit(solution)/shard_map/while/body/eval_jaxpr/ppermute | solution.py:15
  472.7 39.3 %collective-permute-start.4 = (bf16[1,512,12,64]{1,3,2,0:T(8,128)(2,1)}, bf16[1,512,12,64]{1,3,2,0:T(8,128)(2,1)}, u32[]{:S(2)}, u32[]{:S(2)}) collective-permute-start(bf16[1,512,12,64]{1,3,2,0:T(8,128)(2,1)} %convert_element_type.384), channel_id=1, source_target_pairs={{0,4},{4,8},{8,12},{12,16},{16,20},{20,24},{24,28},{28,0},{1,5},{5... | collective-permute-start | bytes 2359304 | tf_op jit(solution)/shard_map/while/body/eval_jaxpr/ppermute | solution.py:15
  472.7 56.1 %collective-permute-start.2 = (bf16[1,512,12,64]{1,3,2,0:T(8,128)(2,1)S(1)}, bf16[1,512,12,64]{1,3,2,0:T(8,128)(2,1)S(1)}, u32[]{:S(2)}, u32[]{:S(2)}) collective-permute-start(bf16[1,512,12,64]{1,3,2,0:T(8,128)(2,1)S(1)} %copy.122), channel_id=1, source_target_pairs={{0,4},{4,8},{8,12},{12,16},{16,20},{20,24},{24,28},{28,0},{1,5},{5... | collective-permute-start | bytes 2359304 | tf_op jit(solution)/shard_map/while/body/eval_jaxpr/ppermute | solution.py:15
  472.7 71.7 %collective-permute-start.3 = (bf16[1,512,12,64]{1,3,2,0:T(8,128)(2,1)}, bf16[1,512,12,64]{1,3,2,0:T(8,128)(2,1)S(1)}, u32[]{:S(2)}, u32[]{:S(2)}) collective-permute-start(bf16[1,512,12,64]{1,3,2,0:T(8,128)(2,1)} %copy.123), channel_id=1, source_target_pairs={{0,4},{4,8},{8,12},{12,16},{16,20},{20,24},{24,28},{28,0},{1,5},{5... | collective-permute-start | bytes 2359304 | tf_op jit(solution)/shard_map/while/body/eval_jaxpr/ppermute | solution.py:15
  570.7 39.4 %collective-permute-start.4 = (bf16[1,512,12,64]{1,3,2,0:T(8,128)(2,1)}, bf16[1,512,12,64]{1,3,2,0:T(8,128)(2,1)}, u32[]{:S(2)}, u32[]{:S(2)}) collective-permute-start(bf16[1,512,12,64]{1,3,2,0:T(8,128)(2,1)} %convert_element_type.384), channel_id=1, source_target_pairs={{0,4},{4,8},{8,12},{12,16},{16,20},{20,24},{24,28},{28,0},{1,5},{5... | collective-permute-start | bytes 2359304 | tf_op jit(solution)/shard_map/while/body/eval_jaxpr/ppermute | solution.py:15
  570.7 56.1 %collective-permute-start.2 = (bf16[1,512,12,64]{1,3,2,0:T(8,128)(2,1)S(1)}, bf16[1,512,12,64]{1,3,2,0:T(8,128)(2,1)S(1)}, u32[]{:S(2)}, u32[]{:S(2)}) collective-permute-start(bf16[1,512,12,64]{1,3,2,0:T(8,128)(2,1)S(1)} %copy.122), channel_id=1, source_target_pairs={{0,4},{4,8},{8,12},{12,16},{16,20},{20,24},{24,28},{28,0},{1,5},{5... | collective-permute-start | bytes 2359304 | tf_op jit(solution)/shard_map/while/body/eval_jaxpr/ppermute | solution.py:15
  570.7 70.8 %collective-permute-start.3 = (bf16[1,512,12,64]{1,3,2,0:T(8,128)(2,1)}, bf16[1,512,12,64]{1,3,2,0:T(8,128)(2,1)S(1)}, u32[]{:S(2)}, u32[]{:S(2)}) collective-permute-start(bf16[1,512,12,64]{1,3,2,0:T(8,128)(2,1)} %copy.123), channel_id=1, source_target_pairs={{0,4},{4,8},{8,12},{12,16},{16,20},{20,24},{24,28},{28,0},{1,5},{5... | collective-permute-start | bytes 2359304 | tf_op jit(solution)/shard_map/while/body/eval_jaxpr/ppermute | solution.py:15
  650.3 39.4 %collective-permute-start.4 = (bf16[1,512,12,64]{1,3,2,0:T(8,128)(2,1)}, bf16[1,512,12,64]{1,3,2,0:T(8,128)(2,1)}, u32[]{:S(2)}, u32[]{:S(2)}) collective-permute-start(bf16[1,512,12,64]{1,3,2,0:T(8,128)(2,1)} %convert_element_type.384), channel_id=1, source_target_pairs={{0,4},{4,8},{8,12},{12,16},{16,20},{20,24},{24,28},{28,0},{1,5},{5... | collective-permute-start | bytes 2359304 | tf_op jit(solution)/shard_map/while/body/eval_jaxpr/ppermute | solution.py:15
  650.3 56.1 %collective-permute-start.2 = (bf16[1,512,12,64]{1,3,2,0:T(8,128)(2,1)S(1)}, bf16[1,512,12,64]{1,3,2,0:T(8,128)(2,1)S(1)}, u32[]{:S(2)}, u32[]{:S(2)}) collective-permute-start(bf16[1,512,12,64]{1,3,2,0:T(8,128)(2,1)S(1)} %copy.122), channel_id=1, source_target_pairs={{0,4},{4,8},{8,12},{12,16},{16,20},{20,24},{24,28},{28,0},{1,5},{5... | collective-permute-start | bytes 2359304 | tf_op jit(solution)/shard_map/while/body/eval_jaxpr/ppermute | solution.py:15
  650.3 69.9 %collective-permute-start.3 = (bf16[1,512,12,64]{1,3,2,0:T(8,128)(2,1)}, bf16[1,512,12,64]{1,3,2,0:T(8,128)(2,1)S(1)}, u32[]{:S(2)}, u32[]{:S(2)}) collective-permute-start(bf16[1,512,12,64]{1,3,2,0:T(8,128)(2,1)} %copy.123), channel_id=1, source_target_pairs={{0,4},{4,8},{8,12},{12,16},{16,20},{20,24},{24,28},{28,0},{1,5},{5... | collective-permute-start | bytes 2359304 | tf_op jit(solution)/shard_map/while/body/eval_jaxpr/ppermute | solution.py:15
  729.0 39.4 %collective-permute-start.4 = (bf16[1,512,12,64]{1,3,2,0:T(8,128)(2,1)}, bf16[1,512,12,64]{1,3,2,0:T(8,128)(2,1)}, u32[]{:S(2)}, u32[]{:S(2)}) collective-permute-start(bf16[1,512,12,64]{1,3,2,0:T(8,128)(2,1)} %convert_element_type.384), channel_id=1, source_target_pairs={{0,4},{4,8},{8,12},{12,16},{16,20},{20,24},{24,28},{28,0},{1,5},{5... | collective-permute-start | bytes 2359304 | tf_op jit(solution)/shard_map/while/body/eval_jaxpr/ppermute | solution.py:15
  729.0 56.1 %collective-permute-start.2 = (bf16[1,512,12,64]{1,3,2,0:T(8,128)(2,1)S(1)}, bf16[1,512,12,64]{1,3,2,0:T(8,128)(2,1)S(1)}, u32[]{:S(2)}, u32[]{:S(2)}) collective-permute-start(bf16[1,512,12,64]{1,3,2,0:T(8,128)(2,1)S(1)} %copy.122), channel_id=1, source_target_pairs={{0,4},{4,8},{8,12},{12,16},{16,20},{20,24},{24,28},{28,0},{1,5},{5... | collective-permute-start | bytes 2359304 | tf_op jit(solution)/shard_map/while/body/eval_jaxpr/ppermute | solution.py:15
  729.0 69.0 %collective-permute-start.3 = (bf16[1,512,12,64]{1,3,2,0:T(8,128)(2,1)}, bf16[1,512,12,64]{1,3,2,0:T(8,128)(2,1)S(1)}, u32[]{:S(2)}, u32[]{:S(2)}) collective-permute-start(bf16[1,512,12,64]{1,3,2,0:T(8,128)(2,1)} %copy.123), channel_id=1, source_target_pairs={{0,4},{4,8},{8,12},{12,16},{16,20},{20,24},{24,28},{28,0},{1,5},{5... | collective-permute-start | bytes 2359304 | tf_op jit(solution)/shard_map/while/body/eval_jaxpr/ppermute | solution.py:15
  806.7 35.4 %collective-permute-start.4 = (bf16[1,512,12,64]{1,3,2,0:T(8,128)(2,1)}, bf16[1,512,12,64]{1,3,2,0:T(8,128)(2,1)}, u32[]{:S(2)}, u32[]{:S(2)}) collective-permute-start(bf16[1,512,12,64]{1,3,2,0:T(8,128)(2,1)} %convert_element_type.384), channel_id=1, source_target_pairs={{0,4},{4,8},{8,12},{12,16},{16,20},{20,24},{24,28},{28,0},{1,5},{5... | collective-permute-start | bytes 2359304 | tf_op jit(solution)/shard_map/while/body/eval_jaxpr/ppermute | solution.py:15
  820.6 38.2 %collective-permute-start.2 = (bf16[1,512,12,64]{1,3,2,0:T(8,128)(2,1)S(1)}, bf16[1,512,12,64]{1,3,2,0:T(8,128)(2,1)S(1)}, u32[]{:S(2)}, u32[]{:S(2)}) collective-permute-start(bf16[1,512,12,64]{1,3,2,0:T(8,128)(2,1)S(1)} %copy.122), channel_id=1, source_target_pairs={{0,4},{4,8},{8,12},{12,16},{16,20},{20,24},{24,28},{28,0},{1,5},{5... | collective-permute-start | bytes 2359304 | tf_op jit(solution)/shard_map/while/body/eval_jaxpr/ppermute | solution.py:15
  820.6 54.3 %collective-permute-start.3 = (bf16[1,512,12,64]{1,3,2,0:T(8,128)(2,1)}, bf16[1,512,12,64]{1,3,2,0:T(8,128)(2,1)S(1)}, u32[]{:S(2)}, u32[]{:S(2)}) collective-permute-start(bf16[1,512,12,64]{1,3,2,0:T(8,128)(2,1)} %copy.123), channel_id=1, source_target_pairs={{0,4},{4,8},{8,12},{12,16},{16,20},{20,24},{24,28},{28,0},{1,5},{5... | collective-permute-start | bytes 2359304 | tf_op jit(solution)/shard_map/while/body/eval_jaxpr/ppermute | solution.py:15
  897.4 34.3 %collective-permute-start.2 = (bf16[1,512,12,64]{1,3,2,0:T(8,128)(2,1)S(1)}, bf16[1,512,12,64]{1,3,2,0:T(8,128)(2,1)S(1)}, u32[]{:S(2)}, u32[]{:S(2)}) collective-permute-start(bf16[1,512,12,64]{1,3,2,0:T(8,128)(2,1)S(1)} %copy.122), channel_id=1, source_target_pairs={{0,4},{4,8},{8,12},{12,16},{16,20},{20,24},{24,28},{28,0},{1,5},{5... | collective-permute-start | bytes 2359304 | tf_op jit(solution)/shard_map/while/body/eval_jaxpr/ppermute | solution.py:15
  897.5 51.1 %collective-permute-start.3 = (bf16[1,512,12,64]{1,3,2,0:T(8,128)(2,1)}, bf16[1,512,12,64]{1,3,2,0:T(8,128)(2,1)S(1)}, u32[]{:S(2)}, u32[]{:S(2)}) collective-permute-start(bf16[1,512,12,64]{1,3,2,0:T(8,128)(2,1)} %copy.123), channel_id=1, source_target_pairs={{0,4},{4,8},{8,12},{12,16},{16,20},{20,24},{24,28},{28,0},{1,5},{5... | collective-permute-start | bytes 2359304 | tf_op jit(solution)/shard_map/while/body/eval_jaxpr/ppermute | solution.py:15
  963.6 32.9 %collective-permute-start.2 = (bf16[1,512,12,64]{1,3,2,0:T(8,128)(2,1)S(1)}, bf16[1,512,12,64]{1,3,2,0:T(8,128)(2,1)S(1)}, u32[]{:S(2)}, u32[]{:S(2)}) collective-permute-start(bf16[1,512,12,64]{1,3,2,0:T(8,128)(2,1)S(1)} %copy.122), channel_id=1, source_target_pairs={{0,4},{4,8},{8,12},{12,16},{16,20},{20,24},{24,28},{28,0},{1,5},{5... | collective-permute-start | bytes 2359304 | tf_op jit(solution)/shard_map/while/body/eval_jaxpr/ppermute | solution.py:15
  963.7 48.1 %collective-permute-start.3 = (bf16[1,512,12,64]{1,3,2,0:T(8,128)(2,1)}, bf16[1,512,12,64]{1,3,2,0:T(8,128)(2,1)S(1)}, u32[]{:S(2)}, u32[]{:S(2)}) collective-permute-start(bf16[1,512,12,64]{1,3,2,0:T(8,128)(2,1)} %copy.123), channel_id=1, source_target_pairs={{0,4},{4,8},{8,12},{12,16},{16,20},{20,24},{24,28},{28,0},{1,5},{5... | collective-permute-start | bytes 2359304 | tf_op jit(solution)/shard_map/while/body/eval_jaxpr/ppermute | solution.py:15
  1019.3 32.2 %collective-permute-start.6 = (bf16[1,512,12,64]{1,3,2,0:T(8,128)(2,1)}, bf16[1,512,12,64]{1,3,2,0:T(8,128)(2,1)}, u32[]{:S(2)}, u32[]{:S(2)}) collective-permute-start(bf16[1,512,12,64]{1,3,2,0:T(8,128)(2,1)} %convert_element_type.253), channel_id=1, source_target_pairs={{0,4},{4,8},{8,12},{12,16},{16,20},{20,24},{24,28},{28,0},{1,5},{5... | collective-permute-start | bytes 2359304 | tf_op jit(solution)/shard_map/ppermute | solution.py:15
  1019.3 32.2 %collective-permute-start.7 = (bf16[1,512,12,64]{1,3,2,0:T(8,128)(2,1)}, bf16[1,512,12,64]{1,3,2,0:T(8,128)(2,1)}, u32[]{:S(2)}, u32[]{:S(2)}) collective-permute-start(bf16[1,512,12,64]{1,3,2,0:T(8,128)(2,1)} %convert_element_type.255), channel_id=1, source_target_pairs={{0,4},{4,8},{8,12},{12,16},{16,20},{20,24},{24,28},{28,0},{1,5},{5... | collective-permute-start | bytes 2359304 | tf_op jit(solution)/shard_map/ppermute | solution.py:15
  1176.9 800.2 %all-gather.17.cloned.1.call-start = ((), (), s32[]{:S(2)}) async-start(), calls=%async_computation.4 | async-start | bytes 7976448 | tf_op jit(solution)/shard_map/all_gather | solution.py:295
  (102 other events, 4320.4 us)
Sparse Core Ops, SparseCore 0:
  9.7 33.6 all-gather.8
  45.0 17.4 all-gather.10
  64.1 37.4 all-gather.12
  103.0 37.4 all-gather.14
  1177.0 333.7 all-reduce.11
  1870.6 106.4 all-gather.16
where the time goes:
time: 2120 us; the launch traced here: 2100 us
  waiting for transfers between devices  1040 us (49%)
  blocking collectives  356 us (17%)
  other arithmetic  259 us (12%)
  local copies, waits for them, and re-layouts  251 us (12%)
  matrix products  112 us (5%)
  starting transfers between devices  58 us (3%)
    ppermute x44, waiting for transfers between devices, passed_along(): lax.ppermute(value, axis, [(i, (i + by) % length) for i in range(length)])  609 us
    unnamed x7, waiting for transfers between devices  335 us
    unnamed x2, blocking collectives  293 us
    unnamed x161, local copies, waits for them, and re-layouts  118 us
    all_gather x1, waiting for transfers between devices, per_device(): lax.all_gather(mine.astype(jnp.bfloat16), 'ctx', axis=0, tiled=True)  95.9 us
    convert_element_type x1, other arithmetic, per_device(): reduced = lax.all_gather(mine.astype(jnp.bfloat16), 'ctx', axis=0, tiled=...  77.3 us
    another operation x1, other arithmetic, per_device(): spread_rows = reduced.reshape(cycle_len, slice_len)  66.6 us
    ppermute x44, starting transfers between devices, passed_along(): lax.ppermute(value, axis, [(i, (i + by) % length) for i in range(length)])  57.8 us
  transfers between devices with their start and end apart: 50, of which 44 were waited for; matrix products, arithmetic and copies ran while one was open for 8% of the time, Pallas kernels for 0%

commit v1 on v0

v1 whole, which is shorter than its diff:
```python
import functools

import jax
import jax.numpy as jnp
from jax import lax
from jax.experimental import pallas as pl
from jax.experimental.pallas import tpu as pltpu
from jax.sharding import PartitionSpec as P

HEADS = 12
HEAD_GROUPS = 2 * HEADS // 3

EPS = 1e-05
NEG = -1e30


def norm_stats(v):
    centered = v - jnp.mean(v, -1, keepdims=True)
    inverse = lax.rsqrt(jnp.mean(centered * centered, -1, keepdims=True) + EPS)
    return (centered * inverse, inverse)


def norm_back(grad_h, normed, inverse, gain):
    grad_normed = grad_h * gain
    return inverse * (
        grad_normed
        - jnp.mean(grad_normed, -1, keepdims=True)
        - normed * jnp.mean(grad_normed * normed, -1, keepdims=True)
    )


def dot_nt(a, b):
    return lax.dot_general(a, b, (((1,), (1,)), ((), ())), preferred_element_type=jnp.float32)


def dot_tn(a, b):
    return lax.dot_general(a, b, (((0,), (0,)), ((), ())), preferred_element_type=jnp.float32)


def dot_nn(a, b):
    return lax.dot_general(a, b, (((1,), (0,)), ((), ())), preferred_element_type=jnp.float32)


def own_lanes(rows, width, side):
    lane = lax.broadcasted_iota(jnp.int32, (rows, width), 1)
    return (lane >= width // 2) == (side == 1)


def load_rows(window_ref, block, padded_ref, side, scale):
    rows, width = window_ref.shape[1:]
    half = rows // 2
    f32 = jnp.float32
    whole = window_ref[block].astype(f32) * scale
    padded_ref[block, :rows, :] = jnp.where(own_lanes(rows, width, side), whole, 0.0).astype(jnp.bfloat16)
    start = pl.multiple_of(side * half, half)
    part = window_ref[block, pl.ds(start, half), :].astype(f32) * scale
    padded_ref[block, rows:, :] = jnp.where(own_lanes(half, width, side), 0.0, part).astype(jnp.bfloat16)


def store_rows(window_ref, block, value, side):
    rows, width = window_ref.shape[1:]
    half = rows // 2
    own = own_lanes(rows, width, side)
    row = lax.broadcasted_iota(jnp.int32, (rows, width), 0)
    mine = (row >= half) == (side == 1)
    shared = jnp.concatenate([value[rows:], value[rows:]], 0)
    shared = jnp.where(mine, shared, 0.0)
    window_ref[block] = jnp.where(own, value[:rows], shared).astype(window_ref.dtype)


def column_chunks(total):
    size = 256 if total % 256 == 0 else total
    return [(at, size) for at in range(0, total, size)]


def visible_pairs(key_meta_ref, query_meta_ref, block, at, size):
    key_place, key_doc = key_meta_ref[0, :, 0:1], key_meta_ref[0, :, 1:2]
    query_place = query_meta_ref[block, 0:1, at : at + size]
    query_doc = query_meta_ref[block, 1:2, at : at + size]
    return (key_place <= query_place) & (key_doc == query_doc)


def attend_kernel(
    kind_ref, side_ref, q_ref, k_ref, v_ref, query_meta_ref, key_meta_ref,
    window_ref, out_ref, log_ref, rows_ref, max_ref, sum_ref, *, scale,
):
    f32 = jnp.float32
    blocks, width, total = out_ref.shape
    key_block = pl.program_id(0)
    side = side_ref[0]

    @pl.when(key_block == 0)
    def _():
        @pl.loop(0, blocks)
        def _(block):
            load_rows(q_ref, block, rows_ref, side, scale)
            max_ref[block] = jnp.full((1, total), NEG, f32)
            sum_ref[block] = jnp.zeros((1, total), f32)
            out_ref[block] = jnp.zeros((width, total), f32)

    def work(block, partial):
        keys, values = k_ref[0], v_ref[0]
        for at, size in column_chunks(total):
            span = slice(at, at + size)
            s = dot_nt(keys, rows_ref[block, span, :])
            if partial:
                visible = visible_pairs(key_meta_ref, query_meta_ref, block, at, size)
                s = jnp.where(visible, s, NEG)
            old_max = max_ref[block, :, span]
            new_max = jnp.maximum(old_max, jnp.max(s, 0, keepdims=True))
            weights = jnp.exp(s - new_max)
            if partial:
                weights = jnp.where(visible, weights, 0.0)
            factor = jnp.exp(old_max - new_max)
            max_ref[block, :, span] = new_max
            sum_ref[block, :, span] = sum_ref[block, :, span] * factor + jnp.sum(weights, 0, keepdims=True)
            added = dot_tn(values, weights.astype(jnp.bfloat16))
            out_ref[block, :, span] = out_ref[block, :, span] * factor + added

    @pl.loop(0, blocks)
    def _(block):
        kind = kind_ref[block * blocks + key_block]

        @pl.when(kind == 1)
        def _():
            work(block, False)

        @pl.when(kind == 2)
        def _():
            work(block, True)

    @pl.when(key_block == blocks - 1)
    def _():
        @pl.loop(0, blocks)
        def _(block):
            total_weight = sum_ref[block]
            out = out_ref[block] / total_weight
            out_ref[block] = out
            log_ref[block] = max_ref[block] + jnp.log(total_weight)
            store_rows(window_ref, block, out.T, side)


def attend_back_kernel(
    kind_ref, side_ref, q_ref, k_ref, v_ref, query_meta_ref, key_meta_ref, grad_ref, out_ref, log_ref,
    grad_q_ref, grad_k_ref, grad_v_ref, rows_ref, grad_rows_ref, delta_ref, sum_q_ref, sum_k_ref, sum_v_ref,
    *, scale,
):
    f32, bf16 = jnp.float32, jnp.bfloat16
    blocks, width, total = out_ref.shape
    key_block = pl.program_id(0)
    side = side_ref[0]

    @pl.when(key_block == 0)
    def _():
        @pl.loop(0, blocks)
        def _(block):
            load_rows(q_ref, block, rows_ref, side, scale)
            load_rows(grad_ref, block, grad_rows_ref, side, 1.0)
            grad_rows = grad_rows_ref[block].astype(f32).T
            delta_ref[block] = jnp.sum(grad_rows * out_ref[block], 0, keepdims=True)
            sum_q_ref[block] = jnp.zeros((width, total), f32)

    sum_k_ref[...] = jnp.zeros_like(sum_k_ref)
    sum_v_ref[...] = jnp.zeros_like(sum_v_ref)

    def work(block, partial):
        keys, values = k_ref[0], v_ref[0]
        for at, size in column_chunks(total):
            span = slice(at, at + size)
            q_rows = rows_ref[block, span, :]
            grad_rows = grad_rows_ref[block, span, :]
            prob = jnp.exp(dot_nt(keys, q_rows) - log_ref[block, :, span])
            if partial:
                visible = visible_pairs(key_meta_ref, query_meta_ref, block, at, size)
                prob = jnp.where(visible, prob, 0.0)
            grad_prob = dot_nt(values, grad_rows)
            sum_v_ref[...] += dot_nn(prob.astype(bf16), grad_rows)
            grad_score = (prob * (grad_prob - delta_ref[block, :, span])).astype(bf16)
            sum_k_ref[...] += dot_nn(grad_score, q_rows)
            sum_q_ref[block, :, span] += dot_tn(keys, grad_score)

    @pl.loop(0, blocks)
    def _(block):
        kind = kind_ref[block * blocks + key_block]

        @pl.when(kind == 1)
        def _():
            work(block, False)

        @pl.when(kind == 2)
        def _():
            work(block, True)

    grad_k_ref[0] = sum_k_ref[...].astype(bf16)
    grad_v_ref[0] = sum_v_ref[...].astype(bf16)

    @pl.when(key_block == blocks - 1)
    def _():
        @pl.loop(0, blocks)
        def _(block):
            store_rows(grad_q_ref, block, sum_q_ref[block].T * scale, side)


def whole_spec(shape, at=0):
    return pl.BlockSpec(shape, lambda i, *_: (0,) * (len(shape) - 1) + (at,))


def attention_calls(blocks, query_len, key_len, width, lanes, scale):
    f32, bf16 = jnp.float32, jnp.bfloat16
    total = query_len + query_len // 2
    shape = jax.ShapeDtypeStruct
    q_spec = whole_spec((blocks, query_len, width), lanes[0])
    block_spec = lambda at: pl.BlockSpec((1, key_len, width), lambda i, *_: (i, 0, at))
    metas = [
        whole_spec((blocks, 2, total)),
        pl.BlockSpec((1, key_len, 2), lambda i, *_: (i, 0, 0)),
    ]
    operands = [q_spec, block_spec(lanes[1]), block_spec(lanes[2])] + metas
    window = whole_spec((blocks, query_len, width))
    columns = whole_spec((blocks, width, total))
    logs = whole_spec((blocks, 1, total))
    params = pltpu.CompilerParams(dimension_semantics=("arbitrary",), vmem_limit_bytes=56 * 1024 * 1024)
    pairs = blocks * (blocks + 1) // 2
    product = 2 * total * key_len * width * pairs
    forward = pl.pallas_call(
        functools.partial(attend_kernel, scale=scale),
        grid_spec=pltpu.PrefetchScalarGridSpec(
            num_scalar_prefetch=2,
            grid=(blocks,),
            in_specs=operands,
            out_specs=[window, columns, logs],
            scratch_shapes=[
                pltpu.VMEM((blocks, total, width), bf16),
                pltpu.VMEM((blocks, 1, total), f32),
                pltpu.VMEM((blocks, 1, total), f32),
            ],
        ),
        out_shape=[
            shape((blocks, query_len, width), bf16),
            shape((blocks, width, total), f32),
            shape((blocks, 1, total), f32),
        ],
        compiler_params=params,
        cost_estimate=pl.CostEstimate(
            flops=8 * product, bytes_accessed=16 << 20, transcendentals=total * key_len * pairs
        ),
        name="attend",
    )
    backward = pl.pallas_call(
        functools.partial(attend_back_kernel, scale=scale),
        grid_spec=pltpu.PrefetchScalarGridSpec(
            num_scalar_prefetch=2,
            grid=(blocks,),
            in_specs=operands + [window, columns, logs],
            out_specs=[window, block_spec(0), block_spec(0)],
            scratch_shapes=[
                pltpu.VMEM((blocks, total, width), bf16),
                pltpu.VMEM((blocks, total, width), bf16),
                pltpu.VMEM((blocks, 1, total), f32),
                pltpu.VMEM((blocks, width, total), f32),
                pltpu.VMEM((key_len, width), f32),
                pltpu.VMEM((key_len, width), f32),
            ],
        ),
        out_shape=[
            shape((blocks, query_len, width), bf16),
            shape((blocks, key_len, width), bf16),
            shape((blocks, key_len, width), bf16),
        ],
        compiler_params=params,
        cost_estimate=pl.CostEstimate(
            flops=20 * product, bytes_accessed=24 << 20, transcendentals=total * key_len * pairs
        ),
        name="attend_back",
    )
    return forward, backward


def swapped(pieces, axis):
    length = len(pieces)
    return [pieces[0]] + [
        lax.ppermute(pieces[k], axis, [(i, i ^ k) for i in range(length)]) for k in range(1, length)
    ]


def per_device(
    tokens,
    positions,
    documents,
    ln1_gain,
    ln1_bias,
    w_qkv,
    bias_qv,
    w_out,
    bias_out,
    ln2_gain,
    ln2_bias,
    w_fc,
    bias_fc,
    w_proj,
    bias_proj,
    cotangent,
):
    f32 = jnp.float32
    bf16 = jnp.bfloat16
    seq_count, block_len, model_width = tokens.shape
    head_dim = model_width // HEADS
    width = 2 * head_dim
    score_scale = float(head_dim) ** (-0.5)
    cycle_len = lax.axis_size("ctx")
    owners = lax.axis_size("fsdp")
    me = lax.axis_index("ctx")
    pieces = cycle_len // HEAD_GROUPS
    pair_wise = pieces == 1
    group, piece = me % HEAD_GROUPS, me // HEAD_GROUPS
    side = group % 2
    query_len = block_len // pieces
    half = query_len // 2
    starts = [3 * head_dim * (j // 2) + head_dim * (j % 2) for j in range(HEAD_GROUPS)]
    forward_call, backward_call = attention_calls(
        cycle_len, query_len, block_len, width, (0, 1, 2) if pair_wise else (0, 0, 1), score_scale
    )

    order = jnp.bitwise_xor(me, jnp.arange(cycle_len)) if pair_wise else jnp.arange(cycle_len)
    ids = lax.all_gather(jnp.concatenate([positions, documents], 0), "ctx", axis=0)[order]
    places, docs = ids[:, 0], ids[:, 1]
    first_place, last_place = places[:, 0], places[:, -1]
    first_doc, last_doc = docs[:, 0], docs[:, -1]
    hidden = (
        (first_place[None, :] > last_place[:, None])
        | (last_doc[None, :] < first_doc[:, None])
        | (first_doc[None, :] > last_doc[:, None])
    )
    full = (
        (last_place[None, :] <= first_place[:, None])
        & (first_doc[None, :] == last_doc[:, None])
        & (last_doc[None, :] == first_doc[:, None])
    )
    kinds = jnp.where(hidden, 0, jnp.where(full, 1, 2)).astype(jnp.int32).reshape(-1)
    own_ids = lax.dynamic_slice_in_dim(ids, piece * query_len, query_len, 2)
    shared_ids = lax.dynamic_slice_in_dim(own_ids, side * half, half, 2)
    query_meta = jnp.concatenate([own_ids, shared_ids], 2)
    key_meta = jnp.swapaxes(ids, 1, 2)
    side_arg = side.reshape(1).astype(jnp.int32)

    def windows(rows):
        return jnp.stack([rows[:, at : at + width] for at in starts])

    def block_at(stacked, j):
        return lax.dynamic_index_in_dim(stacked, j, 0, keepdims=False)

    def query_pieces(stacked):
        return stacked.reshape(HEAD_GROUPS, pieces, query_len, -1).swapaxes(0, 1).reshape(cycle_len, query_len, -1)

    def over_pieces(stacked):
        return jnp.tile(stacked, (pieces, 1, 1))

    def scattered(stacked):
        if pair_wise:
            return jnp.stack(swapped([block_at(stacked, me ^ k) for k in range(cycle_len)], "ctx"))
        return lax.all_to_all(stacked, "ctx", 0, 0, tiled=True)

    def returned(stacked):
        if pair_wise:
            back = jnp.stack(swapped([stacked[k] for k in range(cycle_len)], "ctx"))
            return jnp.stack([block_at(back, me ^ j) for j in range(cycle_len)])
        return lax.all_to_all(stacked, "ctx", 0, 0, tiled=True)

    def joined_queries(back):
        back = back.reshape(pieces, HEAD_GROUPS, query_len, width).swapaxes(0, 1)
        back = back.reshape(HEAD_GROUPS // 2, 2, pieces, 2, half, width)
        lower = back[:, 0, :, 0, :, head_dim:]
        upper = back[:, 1, :, 1, :, :head_dim]
        shared = jnp.stack([lower, upper], 2)
        parts = [back[:, 0, ..., :head_dim], shared, back[:, 1, ..., head_dim:]]
        parts = [part.reshape(HEAD_GROUPS // 2, block_len, head_dim) for part in parts]
        return jnp.concatenate([parts[m][g] for g in range(HEAD_GROUPS // 2) for m in range(3)], 1)

    def joined_keys(back):
        back = back.reshape(pieces, HEAD_GROUPS // 2, 2, block_len, width).astype(f32).sum(0)
        shared = back[:, 0, :, head_dim:] + back[:, 1, :, :head_dim]
        parts = [back[:, 0, :, :head_dim], shared, back[:, 1, :, head_dim:]]
        return jnp.concatenate([parts[m][g] for g in range(HEAD_GROUPS // 2) for m in range(3)], 1).astype(bf16)

    vectors = (ln1_gain, ln1_bias, bias_qv, bias_out, ln2_gain, ln2_bias, bias_fc, bias_proj)
    vector_sizes = [v.size for v in vectors]
    gathered = lax.all_gather(jnp.concatenate(vectors), "fsdp", axis=0).astype(f32)
    cuts = [sum(vector_sizes[:i]) for i in range(len(vectors) + 1)]
    gain_one, shift_one, bqv_all, bout_all, gain_two, shift_two, bfc_all, bproj_all = [
        gathered[:, cuts[i] : cuts[i + 1]].reshape(-1) for i in range(len(vectors))
    ]
    wqkv_all = lax.all_gather(w_qkv, "fsdp", axis=0, tiled=True)
    x = tokens.astype(f32).reshape(-1, model_width)
    normed_one, inverse_one = norm_stats(x)
    h_one = (normed_one * gain_one + shift_one).astype(bf16)
    bias_all = jnp.concatenate(
        [bqv_all[:model_width], jnp.zeros((model_width,), f32), bqv_all[model_width:]]
    )
    qkv = (jnp.dot(h_one, wqkv_all, preferred_element_type=f32) + bias_all).astype(bf16)
    q_windows, k_windows, v_windows = [
        windows(qkv[:, i * model_width : (i + 1) * model_width]) for i in range(3)
    ]
    if pair_wise:
        taken = scattered(jnp.concatenate([q_windows, k_windows, v_windows], -1))
        operands = (taken, taken, taken)
    else:
        taken_q = scattered(query_pieces(q_windows))
        taken_kv = scattered(over_pieces(jnp.concatenate([k_windows, v_windows], -1)))
        operands = (taken_q, taken_kv, taken_kv)
    operands = (kinds, side_arg) + operands + (query_meta, key_meta)
    wfc_all = lax.all_gather(w_fc, "fsdp", axis=0, tiled=True)
    late = lax.all_gather(jnp.concatenate([w_proj, w_out], 0), "fsdp", axis=0)
    wproj_all = late[:, : w_proj.shape[0]].reshape(-1, model_width)
    wout_all = late[:, w_proj.shape[0] :].reshape(-1, model_width)
    out_windows, out_columns, log_total = forward_call(*operands)
    attended_low = joined_queries(returned(out_windows))
    x_two = x + jnp.dot(attended_low, wout_all, preferred_element_type=f32) + bout_all
    normed_two, inverse_two = norm_stats(x_two)
    h_two = (normed_two * gain_two + shift_two).astype(bf16)
    pre_act = jnp.dot(h_two, wfc_all, preferred_element_type=f32) + bfc_all
    activated, gelu_pull = jax.vjp(lambda t: jax.nn.gelu(t, approximate=True), pre_act)
    activated_low = activated.astype(bf16)
    result = x_two + jnp.dot(activated_low, wproj_all, preferred_element_type=f32) + bproj_all
    block_out = result.astype(bf16).reshape(tokens.shape)
    cot_rows = cotangent.reshape(-1, model_width)
    grad_y = cot_rows.astype(f32)
    grad_bproj = jnp.sum(grad_y, 0)
    grad_act = jnp.einsum("td,fd->tf", cot_rows, wproj_all, preferred_element_type=f32)
    grad_pre = gelu_pull(grad_act)[0].astype(bf16)
    grad_bfc = jnp.sum(grad_pre.astype(f32), 0)
    grad_h_two = jnp.einsum("tf,df->td", grad_pre, wfc_all, preferred_element_type=f32)
    grad_g_two = jnp.sum(grad_h_two * normed_two, 0)
    grad_b_two = jnp.sum(grad_h_two, 0)
    grad_x_two = grad_y + norm_back(grad_h_two, normed_two, inverse_two, gain_two)
    grad_branch = grad_x_two.astype(bf16)
    grad_bout = jnp.sum(grad_branch.astype(f32), 0)
    grad_att = jnp.einsum("te,de->td", grad_branch, wout_all, preferred_element_type=f32).astype(bf16)
    taken_grad = scattered(query_pieces(windows(grad_att)))

    def reduced(grad):
        own = lax.psum_scatter(grad, "fsdp", scatter_dimension=0, tiled=True)
        mine = lax.psum_scatter(own, "ctx", scatter_dimension=0, tiled=True)
        return lax.all_gather(mine, "ctx", axis=0, tiled=True).astype(f32)

    grad_wproj = jnp.einsum("tf,td->fd", activated_low, cot_rows, preferred_element_type=f32).astype(bf16)
    grad_wfc = jnp.einsum("td,tf->df", h_two, grad_pre, preferred_element_type=f32).astype(bf16)
    grad_wout = jnp.einsum("td,te->de", attended_low, grad_branch, preferred_element_type=f32).astype(bf16)
    reduced_wproj = reduced(grad_wproj)
    reduced_wfc = reduced(grad_wfc)
    reduced_wout = reduced(grad_wout)

    grad_q_windows, grad_k_windows, grad_v_windows = backward_call(
        *operands, taken_grad, out_columns, log_total
    )
    if pair_wise:
        back = returned(jnp.concatenate([grad_q_windows, grad_k_windows, grad_v_windows], -1))
        back_q, back_k, back_v = [back[..., i * width : (i + 1) * width] for i in range(3)]
    else:
        back_q = returned(grad_q_windows)
        back_kv = returned(jnp.concatenate([grad_k_windows, grad_v_windows], -1))
        back_k, back_v = back_kv[..., :width], back_kv[..., width:]
    grad_q_low, grad_k_low, grad_v_low = joined_queries(back_q), joined_keys(back_k), joined_keys(back_v)
    grad_qkv = jnp.concatenate([grad_q_low, grad_k_low, grad_v_low], -1)
    grad_bqv = jnp.concatenate(
        [jnp.sum(grad_q_low.astype(f32), 0), jnp.sum(grad_v_low.astype(f32), 0)]
    )
    grad_wqkv = jnp.einsum("td,te->de", h_one, grad_qkv, preferred_element_type=f32).astype(bf16)
    grad_h_one = jnp.einsum("te,de->td", grad_qkv, wqkv_all, preferred_element_type=f32)
    grad_g_one = jnp.sum(grad_h_one * normed_one, 0)
    grad_b_one = jnp.sum(grad_h_one, 0)
    grad_x = grad_x_two + norm_back(grad_h_one, normed_one, inverse_one, gain_one)
    grad_tokens = grad_x.astype(bf16).reshape(tokens.shape)

    vector_grads = (grad_g_one, grad_b_one, grad_bqv, grad_bout, grad_g_two, grad_b_two, grad_bfc, grad_bproj)
    packed = jnp.concatenate([grad.reshape(owners, -1) for grad in vector_grads], 1).astype(bf16)
    own_rows = w_qkv.shape[0]
    extra = -(-packed.shape[1] // (own_rows * 128)) * 128
    packed = jnp.pad(packed, ((0, 0), (0, own_rows * extra - packed.shape[1])))
    packed = packed.reshape(owners * own_rows, extra)
    last = reduced(jnp.concatenate([grad_wqkv, packed], 1))
    reduced_wqkv = last[:, : w_qkv.shape[1]]
    reduced_vectors = last[:, w_qkv.shape[1] :].reshape(-1)
    pieces_of = [reduced_vectors[cuts[i] : cuts[i + 1]] for i in range(len(vectors))]
    g_one, b_one, g_bqv, g_bout, g_two, b_two, g_bfc, g_bproj = pieces_of
    return (
        block_out,
        grad_tokens,
        g_one,
        b_one,
        reduced_wqkv,
        g_bqv,
        reduced_wout,
        g_bout,
        g_two,
        b_two,
        reduced_wfc,
        g_bfc,
        reduced_wproj,
        g_bproj,
    )


def solution(mesh):
    return jax.shard_map(
        per_device,
        mesh=mesh,
        in_specs=(
            P("fsdp", "ctx", None),
            P("fsdp", "ctx"),
            P("fsdp", "ctx"),
            P("fsdp"),
            P("fsdp"),
            P("fsdp", None),
            P("fsdp"),
            P("fsdp", None),
            P("fsdp"),
            P("fsdp"),
            P("fsdp"),
            P("fsdp", None),
            P("fsdp"),
            P("fsdp", None),
            P("fsdp"),
            P("fsdp", "ctx", None),
        ),
        out_specs=(
            P("fsdp", "ctx", None),
            P("fsdp", "ctx", None),
            P("fsdp"),
            P("fsdp"),
            P("fsdp", None),
            P("fsdp"),
            P("fsdp", None),
            P("fsdp"),
            P("fsdp"),
            P("fsdp"),
            P("fsdp", None),
            P("fsdp"),
            P("fsdp", None),
            P("fsdp"),
        ),
        check_vma=False,
    )
```

time: 2120 us -> 832 us (0.39)
  waiting for transfers between devices: 1040 us -> 402 us
  blocking collectives: 356 us -> 102 us
  other arithmetic: 259 us -> 26.1 us
  local copies, waits for them, and re-layouts: 251 us -> 88.4 us
  Pallas kernels: 0 us -> 65.4 us
  matrix products: 112 us -> 60.3 us
    ppermute x44 -> x28, waiting for transfers between devices: 609 us -> 77.4 us  [swapped(): lax.ppermute(pieces[k], axis, [(i, i ^ k) for i in range(length)])]
    unnamed x7 -> x14, waiting for transfers between devices: 335 us -> 35.5 us
    unnamed x2 -> x0, blocking collectives: 293 us -> none
    reduce_scatter x0 -> x7, waiting for transfers between devices: none -> 243 us  [the longest x3 182 us: reduced(): mine = lax.psum_scatter(own, 'ctx', scatter_dimension=0, tiled=True)]
    convert_element_type x41 -> x6, other arithmetic: 145 us -> 8.35 us  [the longest x4 6.76 us: reduced(): return lax.all_gather(mine, 'ctx', axis=0, tiled=True).astype(f32)]
    unnamed x161 -> x134, local copies, waits for them, and re-layouts: 118 us -> 39.3 us
    pallas_call x0 -> x2, Pallas kernels: none -> 65.4 us  [the longest x1 34.2 us: per_device(): out_windows, out_columns, log_total = forward_call(*operands)]
    another operation x3 -> x4, other arithmetic: 67.3 us -> 3.21 us  [the longest x1 66.6 us: per_device(): spread_rows = reduced.reshape(cycle_len, slice_len)]
  transfers between devices with their start and end apart: 50 -> 41, of which waited for: 44 -> 17; matrix products, arithmetic and copies ran while one was open for 8% -> 18% of each run, Pallas kernels for 0% -> 8%
where the time goes in v1:
time: 832 us; the launch traced here: 817 us
  waiting for transfers between devices  402 us (48%)
  blocking collectives  102 us (12%)
  local copies, waits for them, and re-layouts  88.4 us (11%)
  Pallas kernels  65.4 us (8%)
  matrix products  60.3 us (7%)
  starting transfers between devices  56.7 us (7%)
  other arithmetic  26.1 us (3%)
  between operations  15.2 us (2%)
    reduce_scatter x3, waiting for transfers between devices, reduced(): mine = lax.psum_scatter(own, 'ctx', scatter_dimension=0, tiled=True)  182 us
    ppermute x28, waiting for transfers between devices, swapped(): lax.ppermute(pieces[k], axis, [(i, i ^ k) for i in range(length)])  77.4 us
    all_gather x2, blocking collectives, reduced(): return lax.all_gather(mine, 'ctx', axis=0, tiled=True).astype(f32)  65 us
    reduce_scatter x4, waiting for transfers between devices, reduced(): own = lax.psum_scatter(grad, 'fsdp', scatter_dimension=0, tiled=True)  60.6 us
    ppermute x28, starting transfers between devices, swapped(): lax.ppermute(pieces[k], axis, [(i, i ^ k) for i in range(length)])  55.4 us
    all_gather x2, waiting for transfers between devices, reduced(): return lax.all_gather(mine, 'ctx', axis=0, tiled=True).astype(f32)  46.7 us
    unnamed x134, local copies, waits for them, and re-layouts  39.3 us
    unnamed x14, waiting for transfers between devices  35.5 us
  transfers between devices with their start and end apart: 41, of which 17 were waited for; matrix products, arithmetic and copies ran while one was open for 18% of the time, Pallas kernels for 8%

profile of v1, /device:TPU:0, one launch (start us, length us, event | category | flops | bytes accessed | tf_op | source)
XLA Modules:
  0.0 817.0 jit_solution(14957771936064559687)
XLA Ops:
  11.7 6.2 all-gather.4
  18.7 31.2 %all-gather.3 = s32[8,2,512]{2,1,0:T(2,128)S(1)} all-gather(s32[1,2,512]{2,1,0:T(2,128)S(1)} %add_bitcast_fusion), channel_id=2, replica_groups=mesh['ctx'=8,'fsdp'=4] {'ctx'}, dimensions={0}, use_global_device_ids=true | all-gather | bytes 36864 | tf_op jit(solution)/shard_map/all_gather | solution.py:325
  51.6 4.6 fusion.10
  82.8 7.2 collective-permute-done.1
  95.1 25.9 %collective-permute-done.3 = bf16[512,384]{1,0:T(8,128)(2,1)S(1)} collective-permute-done((bf16[512,384]{1,0:T(8,128)(2,1)S(1)}, bf16[512,384]{1,0:T(8,128)(2,1)S(1)}, u32[]{:S(2)}, u32[]{:S(2)}) %collective-permute-start.3) | collective-permute-done | bytes 393248 | tf_op jit(solution)/shard_map/ppermute | solution.py:282
  121.8 9.2 %collective-permute-done.4 = bf16[512,384]{1,0:T(8,128)(2,1)S(1)} collective-permute-done((bf16[512,384]{1,0:T(8,128)(2,1)S(1)}, bf16[512,384]{1,0:T(8,128)(2,1)S(1)}, u32[]{:S(2)}, u32[]{:S(2)}) %collective-permute-start.4) | collective-permute-done | bytes 393248 | tf_op jit(solution)/shard_map/ppermute | solution.py:282
  133.4 34.2 %attend.1 = (bf16[8,512,128]{2,1,0:T(8,128)(2,1)}, f32[8,128,768]{2,1,0:T(8,128)}, f32[8,1,768]{2,1,0:T(1,128)}) custom-call(s32[64]{0:T(128)} %reshape.319.kind_ref, s32[1]{0:T(128)} %bitcast.3.side_ref, bf16[8,512,384]{2,1,0:T(8,128)(2,1)} %bitcast_dynamic-update-slice_fusion.7.q_ref.k_ref.v_ref, ...), custom_call_target="tpu_custom_call" | custom-call | flops 28991029248 | bytes 16777216 | tf_op jit(solution)/shard_map/attend/pallas_call | solution.py:415
  169.3 8.5 %collective-permute-start.8 = (bf16[512,128]{1,0:T(8,128)(2,1)S(1)}, bf16[512,128]{1,0:T(8,128)(2,1)S(1)}, u32[]{:S(2)}, u32[]{:S(2)}) collective-permute-start(bf16[512,128]{1,0:T(8,128)(2,1)S(1)} %get-tuple-element.132), channel_id=1, source_target_pairs={{0,8},{4,12},{8,0},{12,4},{16,24},{20,28},{24,16},{28,20},{1,9},{5... | collective-permute-start | bytes 393224 | tf_op jit(solution)/shard_map/ppermute | solution.py:282
  178.9 3.8 collective-permute-start.10
  198.6 5.2 slice.748
  205.1 4.9 fusion.46
  210.1 10.4 %fusion.55 = (bf16[3072]{0:T(1024)(128)(2,1)}, bf16[512,3072]{1,0:T(8,128)(2,1)S(1)}) fusion(f32[512,3072]{1,0:T(8,128)S(1)} %fusion.46, f32[3072]{0:T(1024)S(1)} %add.217, bf16[3072,768]{1,0:T(8,128)(2,1)} %bitcast.441, bf16[1,512,768]{2,1,0:T(8,128)(2,1)S(1)} %copy-done.5), kind=kOutput, calls=%fused_computation.292 | convolution fusion | flops 2450519040 | bytes 14960640 | tf_op jit(solution)/shard_map/td,fd->tf/dot_general | solution.py:428
  222.1 4.8 convolution_convert_fusion.1
  227.2 6.9 multiply_reduce_fusion
  239.6 5.6 convolution_convert_fusion
  266.1 31.2 %attend_back.1 = (bf16[8,512,128]{2,1,0:T(8,128)(2,1)}, bf16[8,512,128]{2,1,0:T(8,128)(2,1)}, bf16[8,512,128]{2,1,0:T(8,128)(2,1)}) custom-call(s32[64]{0:T(128)} %reshape.319.kind_ref, s32[1]{0:T(128)} %bitcast.3.side_ref, bf16[8,512,384]{2,1,0:T(8,128)(2,1)} %bitcast_dynamic-update-slice_fusion.7.q_ref.k_ref.v_ref, ...), custom_call_target="tpu_custom_call" | custom-call | flops 72477573120 | bytes 25165824 | tf_op jit(solution)/shard_map/attend_back/pallas_call | solution.py:452
  319.6 7.6 collective-permute-done.22
  332.8 12.1 %collective-permute-done.24 = bf16[512,384]{1,0:T(8,128)(2,1)S(1)} collective-permute-done((bf16[512,384]{1,0:T(8,128)(2,1)}, bf16[512,384]{1,0:T(8,128)(2,1)S(1)}, u32[]{:S(2)}, u32[]{:S(2)}) %collective-permute-start.24) | collective-permute-done | bytes 393248 | tf_op jit(solution)/shard_map/ppermute | solution.py:282
  345.7 8.0 collective-permute-done.25
  377.7 6.9 concatenate.62
  384.6 6.2 fusion.26
  392.9 3.9 convolution_convert_fusion.2
  401.1 60.5 %reduce-scatter.11.cloned.1.call-done = bf16[192,2432]{1,0:T(8,128)(2,1)} async-done(((bf16[768,2432]{1,0:T(8,128)(2,1)}), bf16[192,2432]{1,0:T(8,128)(2,1)}) %reduce-scatter.11.cloned.1.call-update) | async-done | bytes 933904 | tf_op jit(solution)/shard_map/reduce_scatter | solution.py:441
  461.7 67.4 %reduce-scatter.19.cloned.1.call-done = bf16[24,3072]{1,0:T(8,128)(2,1)} async-done(((bf16[192,3072]{1,0:T(8,128)(2,1)}), bf16[24,3072]{1,0:T(8,128)(2,1)}) %reduce-scatter.19.cloned.1.call-update) | async-done | bytes 147472 | tf_op jit(solution)/shard_map/reduce_scatter | solution.py:442
  529.4 9.5 %fusion.29 = bf16[1,512,768]{2,1,0:T(8,128)(2,1)} fusion(f32[512,768]{1,0:T(8,128)} %copy-done.1, bf16[3072,768]{1,0:T(8,128)(2,1)} %bitcast.442, f32[768]{0:T(1024)S(1)} %add.223, f32[512,3072]{1,0:T(8,128)} %copy-done.34, f32[3072]{0:T(1024)S(1)} %copy-done.16), kind=kOutput, calls=%fused_computation.55 | convolution fusion | flops 2432827392 | bytes 13384704 | tf_op jit(solution)/shard_map/dot_general | solution.py:423
  538.8 56.6 %reduce-scatter.23.cloned.1.call-done = bf16[96,768]{1,0:T(8,128)(2,1)} async-done(((bf16[768,768]{1,0:T(8,128)(2,1)}), bf16[96,768]{1,0:T(8,128)(2,1)}) %reduce-scatter.23.cloned.1.call-update) | async-done | bytes 147472 | tf_op jit(solution)/shard_map/reduce_scatter | solution.py:442
  598.4 57.9 %reduce-scatter.15.cloned.1.call-done = bf16[24,768]{1,0:T(8,128)(2,1)} async-done(((bf16[192,768]{1,0:T(8,128)(2,1)}), bf16[24,768]{1,0:T(8,128)(2,1)}) %reduce-scatter.15.cloned.1.call-update) | async-done | bytes 36880 | tf_op jit(solution)/shard_map/reduce_scatter | solution.py:442
  656.3 31.2 %all_gather.45 = bf16[192,768]{1,0:T(8,128)(2,1)S(1)} all-gather(bf16[24,768]{1,0:T(8,128)(2,1)} %reduce-scatter.15.cloned.1.call-done), channel_id=1, replica_groups=mesh['ctx'=8,'fsdp'=4] {'ctx'}, dimensions={0}, use_global_device_ids=true | all-gather | bytes 331776 | tf_op jit(solution)/shard_map/all_gather | solution.py:443
  688.4 32.2 %reduce-scatter.25.cloned.1.call-done = bf16[24,2432]{1,0:T(8,128)(2,1)} async-done(((bf16[192,2432]{1,0:T(8,128)(2,1)}), bf16[24,2432]{1,0:T(8,128)(2,1)}) %reduce-scatter.25.cloned.1.call-update) | async-done | bytes 116752
  720.5 33.9 %all_gather.44 = bf16[192,2432]{1,0:T(8,128)(2,1)S(1)} all-gather(bf16[24,2432]{1,0:T(8,128)(2,1)} %reduce-scatter.25.cloned.1.call-done), channel_id=1, replica_groups=mesh['ctx'=8,'fsdp'=4] {'ctx'}, dimensions={0}, use_global_device_ids=true | all-gather | bytes 1050624 | tf_op jit(solution)/shard_map/all_gather | solution.py:443
  757.7 7.5 all-gather.15.cloned.1.call-done
  768.2 39.2 %all-gather.17.cloned.1.call-done = bf16[768,768]{1,0:T(8,128)(2,1)} async-done(((bf16[96,768]{1,0:T(8,128)(2,1)}), bf16[768,768]{1,0:T(8,128)(2,1)}) %all-gather.17.cloned.1.call-update) | async-done | bytes 1179664 | tf_op jit(solution)/shard_map/all_gather | solution.py:443
  (317 shorter events, 161.4 us)
Async XLA Ops:
  7.3 44.3 %all-gather.11.cloned.1.call-start = ((), (), s32[]{:S(2)}) async-start(), calls=%async_computation.8 | async-start | bytes 4423680 | tf_op jit(solution)/shard_map/all_gather | solution.py:392
  8.0 189.2 %all-gather.19.cloned.1.call-start = ((), (), s32[]{:S(2)}) async-start(), calls=%async_computation.19 | async-start | bytes 7372800 | tf_op jit(solution)/shard_map/all_gather | solution.py:412
  10.7 194.4 %all-gather.13.cloned.1.call-start = ((), (), s32[]{:S(2)}) async-start(), calls=%async_computation.9 | async-start | bytes 5898240 | tf_op jit(solution)/shard_map/all_gather | solution.py:411
  11.5 387.5 %reduce-scatter.17.cloned.1.call-start = ((), (), s32[]{:S(2)}) async-start(), calls=%async_computation.13 | async-start | bytes 5898240 | tf_op jit(solution)/shard_map/reduce_scatter | solution.py:441
  69.7 20.3 %collective-permute-start.1 = (bf16[512,384]{1,0:T(8,128)(2,1)}, bf16[512,384]{1,0:T(8,128)(2,1)S(1)}, u32[]{:S(2)}, u32[]{:S(2)}) collective-permute-start(bf16[512,384]{1,0:T(8,128)(2,1)} %get-tuple-element.56), channel_id=1, source_target_pairs={{0,8},{4,12},{8,0},{12,4},{16,24},{20,28},{24,16},{28,20},{1,9},{5... | collective-permute-start | bytes 1179656 | tf_op jit(solution)/shard_map/ppermute | solution.py:282
  72.9 21.4 %collective-permute-start.2 = (bf16[512,384]{1,0:T(8,128)(2,1)}, bf16[512,384]{1,0:T(8,128)(2,1)S(1)}, u32[]{:S(2)}, u32[]{:S(2)}) collective-permute-start(bf16[512,384]{1,0:T(8,128)(2,1)} %get-tuple-element.55), channel_id=1, source_target_pairs={{0,12},{4,8},{8,4},{12,0},{16,28},{20,24},{24,20},{28,16},{1,13},{... | collective-permute-start | bytes 1179656 | tf_op jit(solution)/shard_map/ppermute | solution.py:282
  74.9 46.0 %collective-permute-start.3 = (bf16[512,384]{1,0:T(8,128)(2,1)S(1)}, bf16[512,384]{1,0:T(8,128)(2,1)S(1)}, u32[]{:S(2)}, u32[]{:S(2)}) collective-permute-start(bf16[512,384]{1,0:T(8,128)(2,1)S(1)} %get-tuple-element.54), channel_id=1, source_target_pairs={{0,16},{4,20},{8,24},{12,28},{16,0},{20,4},{24,8},{28,12},{1,17},{... | collective-permute-start | bytes 1179656 | tf_op jit(solution)/shard_map/ppermute | solution.py:282
  76.7 54.2 %collective-permute-start.4 = (bf16[512,384]{1,0:T(8,128)(2,1)S(1)}, bf16[512,384]{1,0:T(8,128)(2,1)S(1)}, u32[]{:S(2)}, u32[]{:S(2)}) collective-permute-start(bf16[512,384]{1,0:T(8,128)(2,1)S(1)} %get-tuple-element.53), channel_id=1, source_target_pairs={{0,20},{4,16},{8,28},{12,24},{16,4},{20,0},{24,12},{28,8},{1,21},{... | collective-permute-start | bytes 1179656 | tf_op jit(solution)/shard_map/ppermute | solution.py:282
  78.8 53.0 %collective-permute-start.5 = (bf16[512,384]{1,0:T(8,128)(2,1)S(1)}, bf16[512,384]{1,0:T(8,128)(2,1)S(1)}, u32[]{:S(2)}, u32[]{:S(2)}) collective-permute-start(bf16[512,384]{1,0:T(8,128)(2,1)S(1)} %get-tuple-element.52), channel_id=1, source_target_pairs={{0,24},{4,28},{8,16},{12,20},{16,8},{20,12},{24,0},{28,4},{1,25},{... | collective-permute-start | bytes 1179656 | tf_op jit(solution)/shard_map/ppermute | solution.py:282
  90.0 42.6 %collective-permute-start.6 = (bf16[512,384]{1,0:T(8,128)(2,1)S(1)}, bf16[512,384]{1,0:T(8,128)(2,1)S(1)}, u32[]{:S(2)}, u32[]{:S(2)}) collective-permute-start(bf16[512,384]{1,0:T(8,128)(2,1)S(1)} %get-tuple-element.51), channel_id=1, source_target_pairs={{0,28},{4,24},{8,20},{12,16},{16,12},{20,8},{24,4},{28,0},{1,29},{... | collective-permute-start | bytes 1179656 | tf_op jit(solution)/shard_map/ppermute | solution.py:282
  168.9 13.8 %collective-permute-start.7 = (bf16[512,128]{1,0:T(8,128)(2,1)S(1)}, bf16[512,128]{1,0:T(8,128)(2,1)S(1)}, u32[]{:S(2)}, u32[]{:S(2)}) collective-permute-start(bf16[512,128]{1,0:T(8,128)(2,1)S(1)} %get-tuple-element.133), channel_id=1, source_target_pairs={{0,4},{4,0},{8,12},{12,8},{16,20},{20,16},{24,28},{28,24},{1,5},{5... | collective-permute-start | bytes 393224 | tf_op jit(solution)/shard_map/ppermute | solution.py:282
  169.3 15.8 %collective-permute-start.8 = (bf16[512,128]{1,0:T(8,128)(2,1)S(1)}, bf16[512,128]{1,0:T(8,128)(2,1)S(1)}, u32[]{:S(2)}, u32[]{:S(2)}) collective-permute-start(bf16[512,128]{1,0:T(8,128)(2,1)S(1)} %get-tuple-element.132), channel_id=1, source_target_pairs={{0,8},{4,12},{8,0},{12,4},{16,24},{20,28},{24,16},{28,20},{1,9},{5... | collective-permute-start | bytes 393224 | tf_op jit(solution)/shard_map/ppermute | solution.py:282
  226.9 172.8 %reduce-scatter.21.cloned.1.call-start = ((), (), s32[]{:S(2)}) async-start(), calls=%async_computation.16 | async-start | bytes 5898240 | tf_op jit(solution)/shard_map/reduce_scatter | solution.py:441
  238.7 13.5 %collective-permute-start.14 = (bf16[512,128]{1,0:T(8,128)(2,1)}, bf16[512,128]{1,0:T(8,128)(2,1)}, u32[]{:S(2)}, u32[]{:S(2)}) collective-permute-start(bf16[512,128]{1,0:T(8,128)(2,1)} %get-tuple-element.115), channel_id=1, source_target_pairs={{0,4},{4,0},{8,12},{12,8},{16,20},{20,16},{24,28},{28,24},{1,5},{5... | collective-permute-start | bytes 393224 | tf_op jit(solution)/shard_map/ppermute | solution.py:282
  249.1 12.5 %collective-permute-start.17 = (bf16[512,128]{1,0:T(8,128)(2,1)}, bf16[512,128]{1,0:T(8,128)(2,1)}, u32[]{:S(2)}, u32[]{:S(2)}) collective-permute-start(bf16[512,128]{1,0:T(8,128)(2,1)} %get-tuple-element.112), channel_id=1, source_target_pairs={{0,16},{4,20},{8,24},{12,28},{16,0},{20,4},{24,8},{28,12},{1,17},{... | collective-permute-start | bytes 393224 | tf_op jit(solution)/shard_map/ppermute | solution.py:282
  251.2 12.0 %collective-permute-start.18 = (bf16[512,128]{1,0:T(8,128)(2,1)S(1)}, bf16[512,128]{1,0:T(8,128)(2,1)}, u32[]{:S(2)}, u32[]{:S(2)}) collective-permute-start(bf16[512,128]{1,0:T(8,128)(2,1)S(1)} %get-tuple-element.111), channel_id=1, source_target_pairs={{0,20},{4,16},{8,28},{12,24},{16,4},{20,0},{24,12},{28,8},{1,21},{... | collective-permute-start | bytes 393224 | tf_op jit(solution)/shard_map/ppermute | solution.py:282
  252.2 148.3 %reduce-scatter.13.cloned.1.call-start = ((), (), s32[]{:S(2)}) async-start(), calls=%async_computation.11 | async-start | bytes 1474560 | tf_op jit(solution)/shard_map/reduce_scatter | solution.py:441
  252.3 12.5 %collective-permute-start.19 = (bf16[512,128]{1,0:T(8,128)(2,1)S(1)}, bf16[512,128]{1,0:T(8,128)(2,1)S(1)}, u32[]{:S(2)}, u32[]{:S(2)}) collective-permute-start(bf16[512,128]{1,0:T(8,128)(2,1)S(1)} %get-tuple-element.110), channel_id=1, source_target_pairs={{0,24},{4,28},{8,16},{12,20},{16,8},{20,12},{24,0},{28,4},{1,25},{... | collective-permute-start | bytes 393224 | tf_op jit(solution)/shard_map/ppermute | solution.py:282
  302.1 13.2 %collective-permute-start.21 = (bf16[512,384]{1,0:T(8,128)(2,1)}, bf16[512,384]{1,0:T(8,128)(2,1)}, u32[]{:S(2)}, u32[]{:S(2)}) collective-permute-start(bf16[512,384]{1,0:T(8,128)(2,1)} %get-tuple-element.49), channel_id=1, source_target_pairs={{0,4},{4,0},{8,12},{12,8},{16,20},{20,16},{24,28},{28,24},{1,5},{5... | collective-permute-start | bytes 1179656 | tf_op jit(solution)/shard_map/ppermute | solution.py:282
  304.3 22.9 %collective-permute-start.22 = (bf16[512,384]{1,0:T(8,128)(2,1)}, bf16[512,384]{1,0:T(8,128)(2,1)}, u32[]{:S(2)}, u32[]{:S(2)}) collective-permute-start(bf16[512,384]{1,0:T(8,128)(2,1)} %get-tuple-element.48), channel_id=1, source_target_pairs={{0,8},{4,12},{8,0},{12,4},{16,24},{20,28},{24,16},{28,20},{1,9},{5... | collective-permute-start | bytes 1179656 | tf_op jit(solution)/shard_map/ppermute | solution.py:282
  309.9 151.7 %reduce-scatter.11.cloned.1.call-start = ((), (), s32[]{:S(2)}) async-start(), calls=%async_computation.10 | async-start | bytes 4669440 | tf_op jit(solution)/shard_map/reduce_scatter | solution.py:441
  310.4 21.6 %collective-permute-start.23 = (bf16[512,384]{1,0:T(8,128)(2,1)}, bf16[512,384]{1,0:T(8,128)(2,1)S(1)}, u32[]{:S(2)}, u32[]{:S(2)}) collective-permute-start(bf16[512,384]{1,0:T(8,128)(2,1)} %get-tuple-element.47), channel_id=1, source_target_pairs={{0,12},{4,8},{8,4},{12,0},{16,28},{20,24},{24,20},{28,16},{1,13},{... | collective-permute-start | bytes 1179656 | tf_op jit(solution)/shard_map/ppermute | solution.py:282
  312.2 32.8 %collective-permute-start.24 = (bf16[512,384]{1,0:T(8,128)(2,1)}, bf16[512,384]{1,0:T(8,128)(2,1)S(1)}, u32[]{:S(2)}, u32[]{:S(2)}) collective-permute-start(bf16[512,384]{1,0:T(8,128)(2,1)} %get-tuple-element.46), channel_id=1, source_target_pairs={{0,16},{4,20},{8,24},{12,28},{16,0},{20,4},{24,8},{28,12},{1,17},{... | collective-permute-start | bytes 1179656 | tf_op jit(solution)/shard_map/ppermute | solution.py:282
  313.5 40.2 %collective-permute-start.25 = (bf16[512,384]{1,0:T(8,128)(2,1)}, bf16[512,384]{1,0:T(8,128)(2,1)S(1)}, u32[]{:S(2)}, u32[]{:S(2)}) collective-permute-start(bf16[512,384]{1,0:T(8,128)(2,1)} %get-tuple-element.45), channel_id=1, source_target_pairs={{0,20},{4,16},{8,28},{12,24},{16,4},{20,0},{24,12},{28,8},{1,21},{... | collective-permute-start | bytes 1179656 | tf_op jit(solution)/shard_map/ppermute | solution.py:282
  315.3 39.2 %collective-permute-start.26 = (bf16[512,384]{1,0:T(8,128)(2,1)}, bf16[512,384]{1,0:T(8,128)(2,1)S(1)}, u32[]{:S(2)}, u32[]{:S(2)}) collective-permute-start(bf16[512,384]{1,0:T(8,128)(2,1)} %get-tuple-element.44), channel_id=1, source_target_pairs={{0,24},{4,28},{8,16},{12,20},{16,8},{20,12},{24,0},{28,4},{1,25},{... | collective-permute-start | bytes 1179656 | tf_op jit(solution)/shard_map/ppermute | solution.py:282
  327.2 28.2 %collective-permute-start.27 = (bf16[512,384]{1,0:T(8,128)(2,1)S(1)}, bf16[512,384]{1,0:T(8,128)(2,1)S(1)}, u32[]{:S(2)}, u32[]{:S(2)}) collective-permute-start(bf16[512,384]{1,0:T(8,128)(2,1)S(1)} %get-tuple-element.43), channel_id=1, source_target_pairs={{0,28},{4,24},{8,20},{12,16},{16,12},{20,8},{24,4},{28,0},{1,29},{... | collective-permute-start | bytes 1179656 | tf_op jit(solution)/shard_map/ppermute | solution.py:282
  399.0 130.1 %reduce-scatter.19.cloned.1.call-start = ((), (), s32[]{:S(2)}) async-start(), calls=%async_computation.14 | async-start | bytes 1327104 | tf_op jit(solution)/shard_map/reduce_scatter | solution.py:442
  399.7 195.8 %reduce-scatter.23.cloned.1.call-start = ((), (), s32[]{:S(2)}) async-start(), calls=%async_computation.17 | async-start | bytes 1327104 | tf_op jit(solution)/shard_map/reduce_scatter | solution.py:442
  400.4 255.9 %reduce-scatter.15.cloned.1.call-start = ((), (), s32[]{:S(2)}) async-start(), calls=%async_computation.12 | async-start | bytes 331776 | tf_op jit(solution)/shard_map/reduce_scatter | solution.py:442
  401.0 319.5 %reduce-scatter.25.cloned.1.call-start = ((), (), s32[]{:S(2)}) async-start(), calls=%async_computation.20 | async-start | bytes 1050624
  461.6 303.7 %all-gather.15.cloned.1.call-start = ((), (), s32[]{:S(2)}) async-start(), calls=%async_computation.15 | async-start | bytes 1327104 | tf_op jit(solution)/shard_map/all_gather | solution.py:443
  529.1 278.3 %all-gather.17.cloned.1.call-start = ((), (), s32[]{:S(2)}) async-start(), calls=%async_computation.18 | async-start | bytes 1327104 | tf_op jit(solution)/shard_map/all_gather | solution.py:443
  (47 other events, 675.2 us)
Sparse Core Ops, SparseCore 0:
  9.7 33.4 all-gather.10
  45.3 44.1 all-gather.18
  91.0 37.4 all-gather.12
  227.0 56.2 reduce-scatter.16
  285.9 47.8 reduce-scatter.20
  336.2 25.7 reduce-scatter.12
  399.1 62.4 reduce-scatter.10
  465.0 64.0 reduce-scatter.18
  532.4 63.0 reduce-scatter.22
  598.6 57.6 reduce-scatter.14
  659.7 60.7 reduce-scatter.24
  722.6 42.6 all-gather.14
  767.5 39.8 all-gather.16

commit v2 on v1

--- a/solution.py
+++ b/solution.py
@@ -205,7 +205,7 @@
     return pl.BlockSpec(shape, lambda i, *_: (0,) * (len(shape) - 1) + (at,))
 
 
-def attention_calls(blocks, query_len, key_len, width, lanes, scale):
+def attention_calls(blocks, query_len, key_len, width, lanes, scale, earlier):
     f32, bf16 = jnp.float32, jnp.bfloat16
     total = query_len + query_len // 2
     shape = jax.ShapeDtypeStruct
@@ -247,11 +247,11 @@
         name="attend",
     )
     backward = pl.pallas_call(
-        functools.partial(attend_back_kernel, scale=scale),
+        leading(functools.partial(attend_back_kernel, scale=scale), 10, earlier),
         grid_spec=pltpu.PrefetchScalarGridSpec(
             num_scalar_prefetch=2,
             grid=(blocks,),
-            in_specs=operands + [window, columns, logs],
+            in_specs=operands + [window, columns, logs] + [ANY_SPEC] * earlier,
             out_specs=[window, block_spec(0), block_spec(0)],
             scratch_shapes=[
                 pltpu.VMEM((blocks, total, width), bf16),
@@ -274,6 +274,141 @@
         name="attend_back",
     )
     return forward, backward
+
+
+def mixed(left, right):
+    width = left.shape[1]
+    lane = lax.broadcasted_iota(jnp.int32, left.shape, 1)
+    return jnp.where(lane < width // 2, pltpu.roll(left, width // 2, 1), pltpu.roll(right, width // 2, 1))
+
+
+def leading(kernel, count, earlier):
+    return lambda *refs: kernel(*refs[:count], *refs[count + earlier :])
+
+
+def split_kernel(me_ref, rows_ref, *refs, carried):
+    outs, windows_ref = refs[carried : carried + HEAD_GROUPS], refs[-1]
+    for source, target in zip(refs[:carried], refs[carried + HEAD_GROUPS : -1]):
+        target[...] = source[...]
+    width = 128
+    parts = windows_ref.shape[2] // width
+    per_part = rows_ref.shape[1] // parts
+    for i in range(parts):
+        for t in range(HEAD_GROUPS // 4):
+            at = i * per_part + 3 * width * t
+            low, middle, high = [
+                rows_ref[:, at + m * width : at + (m + 1) * width].astype(jnp.float32) for m in range(3)
+            ]
+            for g, value in enumerate((low, mixed(low, middle), mixed(middle, high), high)):
+                windows_ref[4 * t + g, :, i * width : (i + 1) * width] = value.astype(windows_ref.dtype)
+    for k, out in enumerate(outs):
+        out[...] = windows_ref[jnp.bitwise_xor(me_ref[0], k)]
+
+
+def join_kernel(me_ref, *refs):
+    f32 = jnp.float32
+    ins, (rows_ref, sums_ref, windows_ref) = refs[:HEAD_GROUPS], refs[HEAD_GROUPS:]
+    width = 128
+    parts = windows_ref.shape[2] // width
+    per_part = rows_ref.shape[1] // parts
+    for k, value_ref in enumerate(ins):
+        windows_ref[jnp.bitwise_xor(me_ref[0], k)] = value_ref[...]
+    for i in range(parts):
+        span = slice(i * width, (i + 1) * width)
+        for t in range(HEAD_GROUPS // 4):
+            a, b, c, d = [windows_ref[4 * t + g, :, span].astype(f32) for g in range(4)]
+            lower = lax.broadcasted_iota(jnp.int32, a.shape, 1) < width // 2
+            b, c = pltpu.roll(b, width // 2, 1), pltpu.roll(c, width // 2, 1)
+            values = (
+                a + jnp.where(lower, 0.0, b),
+                jnp.where(lower, b, c),
+                jnp.where(lower, c, 0.0) + d,
+            )
+            for m, value in enumerate(values):
+                at = i * per_part + (3 * t + m) * width
+                value = value.astype(rows_ref.dtype)
+                rows_ref[:, at : at + width] = value
+                sums_ref[:, at : at + width] = jnp.sum(value.astype(f32), 0, keepdims=True)
+
+
+SMEM_SPEC = pl.BlockSpec(memory_space=pltpu.SMEM)
+ANY_SPEC = pl.BlockSpec(memory_space=pl.ANY)
+VMEM_SPEC = pl.BlockSpec(memory_space=pltpu.VMEM)
+LOCAL = pltpu.CompilerParams(vmem_limit_bytes=48 * 1024 * 1024)
+
+
+def split_rows(me, rows, parts, carried):
+    count = rows.shape[0]
+    columns = 128 * parts
+    outs = pl.pallas_call(
+        functools.partial(split_kernel, carried=len(carried)),
+        in_specs=[SMEM_SPEC] + [VMEM_SPEC] * (1 + len(carried)),
+        out_specs=[VMEM_SPEC] * (HEAD_GROUPS + len(carried)),
+        out_shape=[jax.ShapeDtypeStruct((count, columns), rows.dtype)] * HEAD_GROUPS
+        + [jax.ShapeDtypeStruct(array.shape, array.dtype) for array in carried],
+        scratch_shapes=[pltpu.VMEM((HEAD_GROUPS, count, columns), rows.dtype)],
+        compiler_params=LOCAL,
+        cost_estimate=pl.CostEstimate(flops=0, bytes_accessed=4 * rows.size * 2, transcendentals=0),
+        name="split_rows",
+    )(me, rows, *carried)
+    return outs[:HEAD_GROUPS], outs[HEAD_GROUPS:]
+
+
+def add_kernel(kept_ref, received_ref, sum_ref):
+    total = kept_ref[...].astype(jnp.float32) + received_ref[...].astype(jnp.float32)
+    sum_ref[...] = total.astype(sum_ref.dtype)
+
+
+def added_after(kept, received, earlier):
+    return pl.pallas_call(
+        leading(add_kernel, 2, len(earlier)),
+        in_specs=[VMEM_SPEC] * 2 + [ANY_SPEC] * len(earlier),
+        out_specs=VMEM_SPEC,
+        out_shape=jax.ShapeDtypeStruct(kept.shape, kept.dtype),
+        compiler_params=LOCAL,
+        cost_estimate=pl.CostEstimate(flops=0, bytes_accessed=6 * kept.size, transcendentals=0),
+        name="added_after",
+    )(kept, received, *earlier)
+
+
+def pack_kernel(*refs):
+    arrays, outs = refs[:-HEAD_GROUPS], refs[-HEAD_GROUPS:]
+    for k, out in enumerate(outs):
+        for i, array in enumerate(arrays):
+            width = array.shape[2]
+            out[:, i * width : (i + 1) * width] = array[k]
+
+
+def pack_rows(arrays, earlier=()):
+    blocks, count, width = arrays[0].shape
+    shape = jax.ShapeDtypeStruct((count, width * len(arrays)), arrays[0].dtype)
+    return pl.pallas_call(
+        leading(pack_kernel, len(arrays), len(earlier)),
+        in_specs=[VMEM_SPEC] * len(arrays) + [ANY_SPEC] * len(earlier),
+        out_specs=[VMEM_SPEC] * blocks,
+        out_shape=[shape] * blocks,
+        compiler_params=LOCAL,
+        cost_estimate=pl.CostEstimate(flops=0, bytes_accessed=4 * blocks * shape.size, transcendentals=0),
+        name="pack_rows",
+    )(*arrays, *earlier)
+
+
+def join_rows(me, pieces, model_width, earlier=()):
+    count, columns = pieces[0].shape
+    total = model_width * columns // 128
+    return pl.pallas_call(
+        leading(join_kernel, 1 + HEAD_GROUPS, len(earlier)),
+        in_specs=[SMEM_SPEC] + [VMEM_SPEC] * HEAD_GROUPS + [ANY_SPEC] * len(earlier),
+        out_specs=[VMEM_SPEC, VMEM_SPEC],
+        out_shape=[
+            jax.ShapeDtypeStruct((count, total), pieces[0].dtype),
+            jax.ShapeDtypeStruct((1, total), jnp.float32),
+        ],
+        scratch_shapes=[pltpu.VMEM((HEAD_GROUPS, count, columns), pieces[0].dtype)],
+        compiler_params=LOCAL,
+        cost_estimate=pl.CostEstimate(flops=0, bytes_accessed=4 * count * total * 2, transcendentals=0),
+        name="join_rows",
+    )(me, *pieces, *earlier)
 
 
 def swapped(pieces, axis):
@@ -318,29 +453,40 @@
     half = query_len // 2
     starts = [3 * head_dim * (j // 2) + head_dim * (j % 2) for j in range(HEAD_GROUPS)]
     forward_call, backward_call = attention_calls(
-        cycle_len, query_len, block_len, width, (0, 1, 2) if pair_wise else (0, 0, 1), score_scale
+        cycle_len, query_len, block_len, width, (0, 1, 2) if pair_wise else (0, 0, 1), score_scale,
+        4 if pair_wise else 0,
     )
 
-    order = jnp.bitwise_xor(me, jnp.arange(cycle_len)) if pair_wise else jnp.arange(cycle_len)
-    ids = lax.all_gather(jnp.concatenate([positions, documents], 0), "ctx", axis=0)[order]
-    places, docs = ids[:, 0], ids[:, 1]
-    first_place, last_place = places[:, 0], places[:, -1]
-    first_doc, last_doc = docs[:, 0], docs[:, -1]
-    hidden = (
-        (first_place[None, :] > last_place[:, None])
-        | (last_doc[None, :] < first_doc[:, None])
-        | (first_doc[None, :] > last_doc[:, None])
-    )
-    full = (
-        (last_place[None, :] <= first_place[:, None])
-        & (first_doc[None, :] == last_doc[:, None])
-        & (last_doc[None, :] == first_doc[:, None])
-    )
-    kinds = jnp.where(hidden, 0, jnp.where(full, 1, 2)).astype(jnp.int32).reshape(-1)
-    own_ids = lax.dynamic_slice_in_dim(ids, piece * query_len, query_len, 2)
-    shared_ids = lax.dynamic_slice_in_dim(own_ids, side * half, half, 2)
-    query_meta = jnp.concatenate([own_ids, shared_ids], 2)
-    key_meta = jnp.swapaxes(ids, 1, 2)
+    def exchange(value, axis, by):
+        return lax.ppermute(value, axis, [(i, i ^ by) for i in range(lax.axis_size(axis))])
+
+    ids = jnp.stack([positions[0], documents[0]])[None]
+    if pair_wise:
+        by = 1
+        while by < cycle_len:
+            ids = jnp.concatenate([ids, exchange(ids, "ctx", by)], 0)
+            by *= 2
+    else:
+        ids = lax.all_gather(ids[0], "ctx", axis=0)
+    def metas(ids):
+        places, docs = ids[:, 0], ids[:, 1]
+        first_place, last_place = places[:, 0], places[:, -1]
+        first_doc, last_doc = docs[:, 0], docs[:, -1]
+        hidden = (
+            (first_place[None, :] > last_place[:, None])
+            | (last_doc[None, :] < first_doc[:, None])
+            | (first_doc[None, :] > last_doc[:, None])
+        )
+        full = (
+            (last_place[None, :] <= first_place[:, None])
+            & (first_doc[None, :] == last_doc[:, None])
+            & (last_doc[None, :] == first_doc[:, None])
+        )
+        kinds = jnp.where(hidden, 0, jnp.where(full, 1, 2)).astype(jnp.int32).reshape(-1)
+        own_ids = lax.dynamic_slice_in_dim(ids, piece * query_len, query_len, 2)
+        shared_ids = lax.dynamic_slice_in_dim(own_ids, side * half, half, 2)
+        return kinds, jnp.concatenate([own_ids, shared_ids], 2), jnp.swapaxes(ids, 1, 2)
+
     side_arg = side.reshape(1).astype(jnp.int32)
 
     def windows(rows):
@@ -355,15 +501,7 @@
     def over_pieces(stacked):
         return jnp.tile(stacked, (pieces, 1, 1))
 
-    def scattered(stacked):
-        if pair_wise:
-            return jnp.stack(swapped([block_at(stacked, me ^ k) for k in range(cycle_len)], "ctx"))
-        return lax.all_to_all(stacked, "ctx", 0, 0, tiled=True)
-
-    def returned(stacked):
-        if pair_wise:
-            back = jnp.stack(swapped([stacked[k] for k in range(cycle_len)], "ctx"))
-            return jnp.stack([block_at(back, me ^ j) for j in range(cycle_len)])
+    def all_to_all(stacked):
         return lax.all_to_all(stacked, "ctx", 0, 0, tiled=True)
 
     def joined_queries(back):
@@ -390,6 +528,11 @@
         gathered[:, cuts[i] : cuts[i + 1]].reshape(-1) for i in range(len(vectors))
     ]
     wqkv_all = lax.all_gather(w_qkv, "fsdp", axis=0, tiled=True)
+    wfc_all = lax.all_gather(w_fc, "fsdp", axis=0, tiled=True)
+    late = lax.all_gather(jnp.concatenate([w_proj, w_out], 0), "fsdp", axis=0)
+    wproj_all = late[:, : w_proj.shape[0]].reshape(-1, model_width)
+    wout_all = late[:, w_proj.shape[0] :].reshape(-1, model_width)
+    me_arg = me.reshape(1).astype(jnp.int32)
     x = tokens.astype(f32).reshape(-1, model_width)
     normed_one, inverse_one = norm_stats(x)
     h_one = (normed_one * gain_one + shift_one).astype(bf16)
@@ -397,23 +540,27 @@
         [bqv_all[:model_width], jnp.zeros((model_width,), f32), bqv_all[model_width:]]
     )
     qkv = (jnp.dot(h_one, wqkv_all, preferred_element_type=f32) + bias_all).astype(bf16)
-    q_windows, k_windows, v_windows = [
-        windows(qkv[:, i * model_width : (i + 1) * model_width]) for i in range(3)
-    ]
     if pair_wise:
-        taken = scattered(jnp.concatenate([q_windows, k_windows, v_windows], -1))
+        parts, (ids,) = split_rows(me_arg, qkv, 3, (ids,))
+        taken = jnp.stack(swapped(parts, "ctx"))
         operands = (taken, taken, taken)
     else:
-        taken_q = scattered(query_pieces(q_windows))
-        taken_kv = scattered(over_pieces(jnp.concatenate([k_windows, v_windows], -1)))
+        q_windows, k_windows, v_windows = [
+            windows(qkv[:, i * model_width : (i + 1) * model_width]) for i in range(3)
+        ]
+        taken_q = all_to_all(query_pieces(q_windows))
+        taken_kv = all_to_all(over_pieces(jnp.concatenate([k_windows, v_windows], -1)))
         operands = (taken_q, taken_kv, taken_kv)
+    kinds, query_meta, key_meta = metas(ids)
     operands = (kinds, side_arg) + operands + (query_meta, key_meta)
-    wfc_all = lax.all_gather(w_fc, "fsdp", axis=0, tiled=True)
-    late = lax.all_gather(jnp.concatenate([w_proj, w_out], 0), "fsdp", axis=0)
-    wproj_all = late[:, : w_proj.shape[0]].reshape(-1, model_width)
-    wout_all = late[:, w_proj.shape[0] :].reshape(-1, model_width)
     out_windows, out_columns, log_total = forward_call(*operands)
-    attended_low = joined_queries(returned(out_windows))
+    cot_rows = cotangent.reshape(-1, model_width)
+    grad_act = jnp.einsum("td,fd->tf", cot_rows, wproj_all, preferred_element_type=f32)
+    if pair_wise:
+        back = swapped([out_windows[k] for k in range(cycle_len)], "ctx")
+        attended_low, _ = join_rows(me_arg, back, model_width, (wproj_all, wout_all, grad_act))
+    else:
+        attended_low = joined_queries(all_to_all(out_windows))
     x_two = x + jnp.dot(attended_low, wout_all, preferred_element_type=f32) + bout_all
     normed_two, inverse_two = norm_stats(x_two)
     h_two = (normed_two * gain_two + shift_two).astype(bf16)
@@ -422,10 +569,8 @@
     activated_low = activated.astype(bf16)
     result = x_two + jnp.dot(activated_low, wproj_all, preferred_element_type=f32) + bproj_all
     block_out = result.astype(bf16).reshape(tokens.shape)
-    cot_rows = cotangent.reshape(-1, model_width)
     grad_y = cot_rows.astype(f32)
     grad_bproj = jnp.sum(grad_y, 0)
-    grad_act = jnp.einsum("td,fd->tf", cot_rows, wproj_all, preferred_element_type=f32)
     grad_pre = gelu_pull(grad_act)[0].astype(bf16)
     grad_bfc = jnp.sum(grad_pre.astype(f32), 0)
     grad_h_two = jnp.einsum("tf,df->td", grad_pre, wfc_all, preferred_element_type=f32)
@@ -435,36 +580,90 @@
     grad_branch = grad_x_two.astype(bf16)
     grad_bout = jnp.sum(grad_branch.astype(f32), 0)
     grad_att = jnp.einsum("te,de->td", grad_branch, wout_all, preferred_element_type=f32).astype(bf16)
-    taken_grad = scattered(query_pieces(windows(grad_att)))
-
-    def reduced(grad):
-        own = lax.psum_scatter(grad, "fsdp", scatter_dimension=0, tiled=True)
+    row, column = me // 2, me % 2
+    chip, core = lax.axis_index("fsdp") // 2, lax.axis_index("fsdp") % 2
+    rows_apart = cycle_len // 2
+
+    def pick(value, j, axis):
+        return lax.dynamic_index_in_dim(value, j, axis, keepdims=False)
+
+    def added(kept, *others):
+        total = kept.astype(f32)
+        for other in others:
+            total = total + other.astype(f32)
+        return total.astype(bf16)
+
+    def product(left, right):
+        grad = jnp.einsum("tr,tc->rc", left, right, preferred_element_type=f32).astype(bf16)
+        return grad.reshape(owners // 2, 2, -1, grad.shape[1])
+
+    def over_cores(grad):
+        return added(pick(grad, core, 1), exchange(pick(grad, 1 - core, 1), "fsdp", 1))
+
+    def first_parts(a, b):
+        b = b.reshape(2, rows_apart, 2, -1, b.shape[-1])
+        return (pick(a, chip, 0), pick(b, column, 2)), (pick(a, 1 - chip, 0), pick(b, 1 - column, 2))
+
+    def second_parts(kept, sent, earlier=()):
+        a = added_after(kept[0], exchange(sent[0], "fsdp", 2), earlier)
+        b = added_after(kept[1], exchange(sent[1], "ctx", 1), earlier)
+        a = a.reshape(rows_apart, 2, -1, a.shape[-1])
+        return (pick(a, column, 1), pick(b, chip, 0)), (pick(a, 1 - column, 1), pick(b, 1 - chip, 0))
+
+    def third_parts(kept, sent, earlier=()):
+        a = added_after(kept[0], exchange(sent[0], "ctx", 1), earlier)
+        return a, added_after(kept[1], exchange(sent[1], "fsdp", 2), earlier)
+
+    def last_sum(value):
+        return added(
+            pick(value, row, 0), *[exchange(pick(value, row ^ k, 0), "ctx", 2 * k) for k in range(1, rows_apart)]
+        )
+
+    def spread(mine):
+        around = jnp.stack([mine] + [exchange(mine, "ctx", 2 * k) for k in range(1, rows_apart)])
+        around = jnp.stack([pick(around, row ^ j, 0) for j in range(rows_apart)])
+        both = jnp.stack([around, exchange(around, "ctx", 1)])
+        both = jnp.stack([pick(both, column ^ j, 0) for j in range(2)], 1)
+        return both.reshape(-1, mine.shape[-1])
+
+    def over_ctx(pair):
+        own = added(pick(pair, chip, 0), exchange(pick(pair, 1 - chip, 0), "fsdp", 2))
         mine = lax.psum_scatter(own, "ctx", scatter_dimension=0, tiled=True)
-        return lax.all_gather(mine, "ctx", axis=0, tiled=True).astype(f32)
-
-    grad_wproj = jnp.einsum("tf,td->fd", activated_low, cot_rows, preferred_element_type=f32).astype(bf16)
-    grad_wfc = jnp.einsum("td,tf->df", h_two, grad_pre, preferred_element_type=f32).astype(bf16)
-    grad_wout = jnp.einsum("td,te->de", attended_low, grad_branch, preferred_element_type=f32).astype(bf16)
-    reduced_wproj = reduced(grad_wproj)
-    reduced_wfc = reduced(grad_wfc)
-    reduced_wout = reduced(grad_wout)
+        return lax.all_gather(mine, "ctx", axis=0, tiled=True)
+
+    def early_sums(cot_rows, h_two, attended_low):
+        early = [
+            over_cores(product(left, right))
+            for left, right in ((activated_low, cot_rows), (h_two, grad_pre), (attended_low, grad_branch))
+        ]
+        return early[0], jnp.concatenate(early[1:], -1)
+
+    if pair_wise:
+        parts, carried = split_rows(me_arg, grad_att, 1, (cot_rows, h_two, attended_low))
+        taken_grad = jnp.stack(swapped(parts, "ctx"))
+        early = first_parts(*early_sums(*carried))
+        earlier = (*early[0], *early[1])
+    else:
+        taken_grad = all_to_all(query_pieces(windows(grad_att)))
+        early = [over_ctx(pair) for pair in early_sums(cot_rows, h_two, attended_low)]
+        earlier = ()
 
     grad_q_windows, grad_k_windows, grad_v_windows = backward_call(
-        *operands, taken_grad, out_columns, log_total
+        *operands, taken_grad, out_columns, log_total, *earlier
     )
     if pair_wise:
-        back = returned(jnp.concatenate([grad_q_windows, grad_k_windows, grad_v_windows], -1))
-        back_q, back_k, back_v = [back[..., i * width : (i + 1) * width] for i in range(3)]
+        back = swapped(pack_rows((grad_q_windows, grad_k_windows, grad_v_windows)), "ctx")
+        early = second_parts(*early, (grad_q_windows,))
+        grad_qkv, grad_sums = join_rows(me_arg, back, model_width)
+        early = [spread(last_sum(value)) for value in third_parts(*early, (grad_qkv,))]
+        grad_sums = grad_sums[0]
     else:
-        back_q = returned(grad_q_windows)
-        back_kv = returned(jnp.concatenate([grad_k_windows, grad_v_windows], -1))
-        back_k, back_v = back_kv[..., :width], back_kv[..., width:]
-    grad_q_low, grad_k_low, grad_v_low = joined_queries(back_q), joined_keys(back_k), joined_keys(back_v)
-    grad_qkv = jnp.concatenate([grad_q_low, grad_k_low, grad_v_low], -1)
-    grad_bqv = jnp.concatenate(
-        [jnp.sum(grad_q_low.astype(f32), 0), jnp.sum(grad_v_low.astype(f32), 0)]
-    )
-    grad_wqkv = jnp.einsum("td,te->de", h_one, grad_qkv, preferred_element_type=f32).astype(bf16)
+        back_q = all_to_all(grad_q_windows)
+        back_kv = all_to_all(jnp.concatenate([grad_k_windows, grad_v_windows], -1))
+        grad_k_low, grad_v_low = joined_keys(back_kv[..., :width]), joined_keys(back_kv[..., width:])
+        grad_qkv = jnp.concatenate([joined_queries(back_q), grad_k_low, grad_v_low], -1)
+        grad_sums = jnp.sum(grad_qkv.astype(f32), 0)
+    grad_bqv = jnp.concatenate([grad_sums[:model_width], grad_sums[2 * model_width :]])
     grad_h_one = jnp.einsum("te,de->td", grad_qkv, wqkv_all, preferred_element_type=f32)
     grad_g_one = jnp.sum(grad_h_one * normed_one, 0)
     grad_b_one = jnp.sum(grad_h_one, 0)
@@ -476,8 +675,18 @@
     own_rows = w_qkv.shape[0]
     extra = -(-packed.shape[1] // (own_rows * 128)) * 128
     packed = jnp.pad(packed, ((0, 0), (0, own_rows * extra - packed.shape[1])))
-    packed = packed.reshape(owners * own_rows, extra)
-    last = reduced(jnp.concatenate([grad_wqkv, packed], 1))
+    packed = packed.reshape(owners // 2, 2, own_rows, extra)
+    last = over_cores(jnp.concatenate([product(h_one, grad_qkv), packed], -1))
+    if pair_wise:
+        cut = w_qkv.shape[1] // 256 * 128
+        last = third_parts(*second_parts(*first_parts(last[..., :cut], last[..., cut:])))
+        last = spread(last_sum(jnp.concatenate(last, -1)))
+    else:
+        last = over_ctx(last)
+    last = last.astype(f32)
+    early = [value.astype(f32) for value in early]
+    reduced_wproj = early[0]
+    reduced_wfc, reduced_wout = early[1][:, : w_fc.shape[1]], early[1][:, w_fc.shape[1] :]
     reduced_wqkv = last[:, : w_qkv.shape[1]]
     reduced_vectors = last[:, w_qkv.shape[1] :].reshape(-1)
     pieces_of = [reduced_vectors[cuts[i] : cuts[i + 1]] for i in range(len(vectors))]

time: 832 us -> 534 us (0.64)
  waiting for transfers between devices: 402 us -> 173 us
  blocking collectives: 102 us -> 5.2 us
  starting transfers between devices: 56.7 us -> 133 us
  local copies, waits for them, and re-layouts: 88.4 us -> 46 us
  Pallas kernels: 65.4 us -> 83.1 us
  other arithmetic: 26.1 us -> 17.3 us
    reduce_scatter x7 -> x0, waiting for transfers between devices: 243 us -> none  [the longest x3 182 us: reduced(): mine = lax.psum_scatter(own, 'ctx', scatter_dimension=0, tiled=True)]
    all_gather x3 -> x0, blocking collectives: 96.2 us -> none  [the longest x2 65 us: reduced(): return lax.all_gather(mine, 'ctx', axis=0, tiled=True).astype(f32)]
    ppermute x0 -> x36, starting transfers between devices: none -> 68 us  [exchange(): lax.ppermute(value, axis, [(i, i ^ by) for i in range(lax.axis_size(axis))])]
    ppermute x0 -> x36, waiting for transfers between devices: none -> 64.7 us  [exchange(): lax.ppermute(value, axis, [(i, i ^ by) for i in range(lax.axis_size(axis))])]
    all_gather x2 -> x0, waiting for transfers between devices: 46.7 us -> none  [reduced(): return lax.all_gather(mine, 'ctx', axis=0, tiled=True).astype(f32)]
    unnamed x14 -> x3, waiting for transfers between devices: 35.5 us -> 0.71 us
    unnamed x134 -> x142, local copies, waits for them, and re-layouts: 39.3 us -> 18 us
    concatenate x7 -> x2, local copies, waits for them, and re-layouts: 16.5 us -> 0.04 us  [per_device(): jnp.concatenate([grad_sums[:model_width], grad_sums[2 * model_width:]])]
  transfers between devices with their start and end apart: 41 -> 67, of which waited for: 17 -> 29; matrix products, arithmetic and copies ran while one was open for 18% -> 14% of each run, Pallas kernels for 8% -> 9%
where the time goes in v2:
time: 534 us; the launch traced here: 527 us
  waiting for transfers between devices  173 us (32%)
  starting transfers between devices  133 us (25%)
  Pallas kernels  83.1 us (16%)
  matrix products  53.7 us (10%)
  local copies, waits for them, and re-layouts  46 us (9%)
  other arithmetic  17.3 us (3%)
  between operations  15.5 us (3%)
    ppermute x28, waiting for transfers between devices, swapped(): lax.ppermute(pieces[k], axis, [(i, i ^ k) for i in range(length)])  93.6 us
    ppermute x36, starting transfers between devices, exchange(): lax.ppermute(value, axis, [(i, i ^ by) for i in range(lax.axis_size(axis))])  68 us
    ppermute x28, starting transfers between devices, swapped(): lax.ppermute(pieces[k], axis, [(i, i ^ k) for i in range(length)])  64.9 us
    ppermute x36, waiting for transfers between devices, exchange(): lax.ppermute(value, axis, [(i, i ^ by) for i in range(lax.axis_size(axis))])  64.7 us
    pallas_call x1, Pallas kernels, per_device(): out_windows, out_columns, log_total = forward_call(*operands)  37.4 us
    pallas_call x1, Pallas kernels, per_device(): backward_call(*operands, taken_grad, out_columns, log_total, *earlier)  33.9 us
    unnamed x142, local copies, waits for them, and re-layouts  18 us
    all_gather x1, waiting for transfers between devices, per_device(): wqkv_all = lax.all_gather(w_qkv, 'fsdp', axis=0, tiled=True)  14.2 us
  transfers between devices with their start and end apart: 67, of which 29 were waited for; matrix products, arithmetic and copies ran while one was open for 14% of the time, Pallas kernels for 9%

profile of v2, /device:TPU:0, one launch (start us, length us, event | category | flops | bytes accessed | tf_op | source)
XLA Modules:
  0.0 526.9 jit_solution(8275890158693194743)
XLA Ops:
  14.1 5.2 all-gather.2
  28.9 14.2 %all-gather.7.cloned.1.call-done = bf16[768,2304]{1,0:T(8,128)(2,1)} async-done(((bf16[192,2304]{1,0:T(8,128)(2,1)}), bf16[768,2304]{1,0:T(8,128)(2,1)}) %all-gather.7.cloned.1.call-update) | async-done | bytes 3538960 | tf_op jit(solution)/shard_map/all_gather | solution.py:530
  43.1 4.2 fusion.9.rows_ref
  65.9 14.6 %collective-permute-done.4 = bf16[512,384]{1,0:T(8,128)(2,1)S(1)} collective-permute-done((bf16[512,384]{1,0:T(8,128)(2,1)S(1)}, bf16[512,384]{1,0:T(8,128)(2,1)S(1)}, u32[]{:S(2)}, u32[]{:S(2)}) %collective-permute-start.4) | collective-permute-done | bytes 393248 | tf_op jit(solution)/shard_map/ppermute | solution.py:417
  81.7 5.8 %collective-permute-done.5 = bf16[512,384]{1,0:T(8,128)(2,1)S(1)} collective-permute-done((bf16[512,384]{1,0:T(8,128)(2,1)S(1)}, bf16[512,384]{1,0:T(8,128)(2,1)S(1)}, u32[]{:S(2)}, u32[]{:S(2)}) %collective-permute-start.5) | collective-permute-done | bytes 393248 | tf_op jit(solution)/shard_map/ppermute | solution.py:417
  87.7 23.1 %collective-permute-done.7 = bf16[512,384]{1,0:T(8,128)(2,1)S(1)} collective-permute-done((bf16[512,384]{1,0:T(8,128)(2,1)S(1)}, bf16[512,384]{1,0:T(8,128)(2,1)S(1)}, u32[]{:S(2)}, u32[]{:S(2)}) %collective-permute-start.7) | collective-permute-done | bytes 393248 | tf_op jit(solution)/shard_map/ppermute | solution.py:417
  112.7 37.4 %attend.1 = (bf16[8,512,128]{2,1,0:T(8,128)(2,1)}, f32[8,128,768]{2,1,0:T(8,128)}, f32[8,1,768]{2,1,0:T(1,128)}) custom-call(s32[64]{0:T(128)} %reshape.256.kind_ref.refs_0_, s32[1]{0:T(128)} %bitcast.3.side_ref.refs_1_, bf16[8,512,384]{2,1,0:T(8,128)(2,1)} %copy-done.30, bf16[8,512,384]{2,1,0:T(8,128)(2,1)} %copy-done.30, bf16[8,512,384]{2,1,0:T(8,128)(2,1)} %copy-done.30, ...), custom_call_target="tpu_custom_call" | custom-call | flops 28991029248 | bytes 16777216 | tf_op jit(solution)/shard_map/attend/pallas_call | solution.py:556
  152.1 15.7 %collective-permute-start.11 = (bf16[512,128]{1,0:T(8,128)(2,1)S(1)}, bf16[512,128]{1,0:T(8,128)(2,1)S(1)}, u32[]{:S(2)}, u32[]{:S(2)}) collective-permute-start(bf16[512,128]{1,0:T(8,128)(2,1)S(1)} %get-tuple-element.123), channel_id=1, source_target_pairs={{0,8},{4,12},{8,0},{12,4},{16,24},{20,28},{24,16},{28,20},{1,9},{5... | collective-permute-start | bytes 393224 | tf_op jit(solution)/shard_map/ppermute | solution.py:417
  169.6 3.9 collective-permute-start.13
  181.0 4.6 convolution_bitcast_fusion.refs_11_
  194.3 12.8 %fusion.73 = (bf16[3072]{0:T(1024)(128)(2,1)}, bf16[512,3072]{1,0:T(8,128)(2,1)S(1)}, f32[512,3072]{1,0:T(8,128)}) fusion(f32[512,3072]{1,0:T(8,128)} %convolution_bitcast_fusion.refs_11_, f32[3072]{0:T(1024)S(1)} %copy-done.37, bf16[512,768]{1,0:T(8,128)(2,1)S(1)} %add_convert_fusion.1.refs_1_, bf16[768,3072]{1,0:T(8,128)(2,1)} %all-gather.9.cloned.1.call-done), kind=kOutput, calls=%fused_computation.228 | convolution fusion | flops 2450519040 | bytes 21252096 | tf_op jit(solution)/shard_map/dot_general | solution.py:567
  215.9 4.3 collective-permute-start.18
  226.8 4.1 convolution_convert_fusion.2
  237.0 9.8 %collective-permute-done.21 = bf16[512,128]{1,0:T(8,128)(2,1)S(1)} collective-permute-done((bf16[512,128]{1,0:T(8,128)(2,1)S(1)}, bf16[512,128]{1,0:T(8,128)(2,1)S(1)}, u32[]{:S(2)}, u32[]{:S(2)}) %collective-permute-start.21) | collective-permute-done | bytes 131104 | tf_op jit(solution)/shard_map/ppermute | solution.py:417
  254.2 33.9 %attend_back.1 = (bf16[8,512,128]{2,1,0:T(8,128)(2,1)}, bf16[8,512,128]{2,1,0:T(8,128)(2,1)}, bf16[8,512,128]{2,1,0:T(8,128)(2,1)}) custom-call(s32[64]{0:T(128)} %reshape.256.kind_ref.refs_0_, s32[1]{0:T(128)} %bitcast.3.side_ref.refs_1_, bf16[8,512,384]{2,1,0:T(8,128)(2,1)} %copy-done.30, bf16[8,512,384]{2,1,0:T(8,128)(2,1)} %copy-done.30, ...), custom_call_target="tpu_custom_call" | custom-call | flops 72477573120 | bytes 25165824 | tf_op jit(solution)/shard_map/attend_back/pallas_call | solution.py:651
  295.4 4.2 collective-permute-start.28
  307.0 17.7 %collective-permute-done.28.refs_3_ = bf16[512,384]{1,0:T(8,128)(2,1)S(1)} collective-permute-done((bf16[512,384]{1,0:T(8,128)(2,1)S(1)}, bf16[512,384]{1,0:T(8,128)(2,1)S(1)}, u32[]{:S(2)}, u32[]{:S(2)}) %collective-permute-start.28) | collective-permute-done | bytes 393248 | tf_op jit(solution)/shard_map/ppermute | solution.py:417
  326.3 9.4 %fusion.33 = bf16[1,512,768]{2,1,0:T(8,128)(2,1)} fusion(f32[512,768]{1,0:T(8,128)} %copy-done.24, bf16[3072,768]{1,0:T(8,128)(2,1)} %bitcast.302, f32[768]{0:T(1024)S(1)} %add.273, f32[512,3072]{1,0:T(8,128)} %get-tuple-element.181, f32[3072]{0:T(1024)S(1)} %copy-done.38), kind=kOutput, calls=%fused_computation.77 | convolution fusion | flops 2432827392 | bytes 13384704 | tf_op jit(solution)/shard_map/dot_general | solution.py:570
  341.5 15.0 %collective-permute-done.31.refs_6_ = bf16[512,384]{1,0:T(8,128)(2,1)S(1)} collective-permute-done((bf16[512,384]{1,0:T(8,128)(2,1)}, bf16[512,384]{1,0:T(8,128)(2,1)S(1)}, u32[]{:S(2)}, u32[]{:S(2)}) %collective-permute-start.31) | collective-permute-done | bytes 393248 | tf_op jit(solution)/shard_map/ppermute | solution.py:417
  367.5 6.2 %fusion.30 = (bf16[768]{0:T(1024)(128)(2,1)}, f32[512]{0:T(512)}, f32[512]{0:T(512)}, bf16[768]{0:T(1024)(128)(2,1)}, f32[512,768]{1,0:T(8,128)}) fusion(bf16[1,512,768]{2,1,0:T(8,128)(2,1)} %param.16, f32[512]{0:T(512)} %copy-done.39, f32[512]{0:T(512)S(1)} %copy-done.32, f32[768]{0:T(1024)} %copy-done.35, ...), kind=kOutput, calls=%fused_computation.54 | convolution fusion | flops 1815868928 | bytes 8271872 | tf_op jit(solution)/shard_map/te,de->td/dot_general | solution.py:667
  387.3 7.3 %collective-permute-done.56.refs_1_ = bf16[4,96,768]{2,1,0:T(8,128)(2,1)S(1)} collective-permute-done((bf16[4,96,768]{2,1,0:T(8,128)(2,1)S(1)}, bf16[4,96,768]{2,1,0:T(8,128)(2,1)S(1)}, u32[]{:S(2)}, u32[]{:S(2)}) %collective-permute-start.56) | collective-permute-done | bytes 589856 | tf_op jit(solution)/shard_map/ppermute | solution.py:461
  396.8 15.6 %collective-permute-start.58 = (bf16[96,768]{1,0:T(8,128)(2,1)S(1)}, bf16[96,768]{1,0:T(8,128)(2,1)S(1)}, u32[]{:S(2)}, u32[]{:S(2)}) collective-permute-start(bf16[96,768]{1,0:T(8,128)(2,1)S(1)} %get-tuple-element.149), channel_id=1, source_target_pairs={{0,16},{4,20},{8,24},{12,28},{16,0},{20,4},{24,8},{28,12},{1,17},{... | collective-permute-start | bytes 442376 | tf_op jit(solution)/shard_map/ppermute | solution.py:461
  415.8 5.0 collective-permute-done.58
  428.6 4.5 collective-permute-done.61
  443.8 6.8 %collective-permute-done.49 = bf16[24,3840]{1,0:T(8,128)(2,1)S(1)} collective-permute-done((bf16[24,3840]{1,0:T(8,128)(2,1)S(1)}, bf16[24,3840]{1,0:T(8,128)(2,1)S(1)}, u32[]{:S(2)}, u32[]{:S(2)}) %collective-permute-start.49) | collective-permute-done | bytes 184352 | tf_op jit(solution)/shard_map/ppermute | solution.py:461
  455.2 4.9 collective-permute-done.53
  460.1 6.2 %collective-permute-start.35 = (bf16[192,1152]{1,0:T(8,128)(2,1)S(1)}, bf16[192,1152]{1,0:T(8,128)(2,1)S(1)}, u32[]{:S(2)}, u32[]{:S(2)}) collective-permute-start(bf16[192,1152]{1,0:T(8,128)(2,1)S(1)} %get-tuple-element.130), channel_id=1, source_target_pairs={{0,2},{1,3},{2,0},{3,1},{4,6},{5,7},{6,4},{7,5},{8,10},{9,11},{10,... | collective-permute-start | bytes 1327112 | tf_op jit(solution)/shard_map/ppermute | solution.py:461
  467.0 6.8 %collective-permute-done.35.refs_1_ = bf16[192,1152]{1,0:T(8,128)(2,1)S(1)} collective-permute-done((bf16[192,1152]{1,0:T(8,128)(2,1)S(1)}, bf16[192,1152]{1,0:T(8,128)(2,1)S(1)}, u32[]{:S(2)}, u32[]{:S(2)}) %collective-permute-start.35) | collective-permute-done | bytes 442400 | tf_op jit(solution)/shard_map/ppermute | solution.py:461
  478.7 3.6 collective-permute-done.36.refs_1_
  484.3 3.6 collective-permute-start.40
  489.2 8.7 %collective-permute-done.40 = bf16[24,2432]{1,0:T(8,128)(2,1)S(1)} collective-permute-done((bf16[24,2432]{1,0:T(8,128)(2,1)S(1)}, bf16[24,2432]{1,0:T(8,128)(2,1)S(1)}, u32[]{:S(2)}, u32[]{:S(2)}) %collective-permute-start.40) | collective-permute-done | bytes 116768 | tf_op jit(solution)/shard_map/ppermute | solution.py:461
  512.5 3.6 collective-permute-done.45
  (386 shorter events, 189.1 us)
Async XLA Ops:
  7.2 35.9 %all-gather.7.cloned.1.call-start = ((), (), s32[]{:S(2)}) async-start(), calls=%async_computation | async-start | bytes 4423680 | tf_op jit(solution)/shard_map/all_gather | solution.py:530
  8.0 165.5 %all-gather.11.cloned.1.call-start = ((), (), s32[]{:S(2)}) async-start(), calls=%async_computation.2 | async-start | bytes 7372800 | tf_op jit(solution)/shard_map/all_gather | solution.py:532
  10.8 183.5 %all-gather.9.cloned.1.call-start = ((), (), s32[]{:S(2)}) async-start(), calls=%async_computation.1 | async-start | bytes 5898240 | tf_op jit(solution)/shard_map/all_gather | solution.py:531
  52.8 27.8 %collective-permute-start.4 = (bf16[512,384]{1,0:T(8,128)(2,1)S(1)}, bf16[512,384]{1,0:T(8,128)(2,1)S(1)}, u32[]{:S(2)}, u32[]{:S(2)}) collective-permute-start(bf16[512,384]{1,0:T(8,128)(2,1)S(1)} %get-tuple-element.54), channel_id=1, source_target_pairs={{0,8},{4,12},{8,0},{12,4},{16,24},{20,28},{24,16},{28,20},{1,9},{5... | collective-permute-start | bytes 1179656 | tf_op jit(solution)/shard_map/ppermute | solution.py:417
  54.2 33.3 %collective-permute-start.5 = (bf16[512,384]{1,0:T(8,128)(2,1)S(1)}, bf16[512,384]{1,0:T(8,128)(2,1)S(1)}, u32[]{:S(2)}, u32[]{:S(2)}) collective-permute-start(bf16[512,384]{1,0:T(8,128)(2,1)S(1)} %get-tuple-element.55), channel_id=1, source_target_pairs={{0,12},{4,8},{8,4},{12,0},{16,28},{20,24},{24,20},{28,16},{1,13},{... | collective-permute-start | bytes 1179656 | tf_op jit(solution)/shard_map/ppermute | solution.py:417
  54.8 32.8 %collective-permute-start.6 = (bf16[512,384]{1,0:T(8,128)(2,1)S(1)}, bf16[512,384]{1,0:T(8,128)(2,1)S(1)}, u32[]{:S(2)}, u32[]{:S(2)}) collective-permute-start(bf16[512,384]{1,0:T(8,128)(2,1)S(1)} %get-tuple-element.56), channel_id=1, source_target_pairs={{0,16},{4,20},{8,24},{12,28},{16,0},{20,4},{24,8},{28,12},{1,17},{... | collective-permute-start | bytes 1179656 | tf_op jit(solution)/shard_map/ppermute | solution.py:417
  57.2 53.6 %collective-permute-start.7 = (bf16[512,384]{1,0:T(8,128)(2,1)S(1)}, bf16[512,384]{1,0:T(8,128)(2,1)S(1)}, u32[]{:S(2)}, u32[]{:S(2)}) collective-permute-start(bf16[512,384]{1,0:T(8,128)(2,1)S(1)} %get-tuple-element.57), channel_id=1, source_target_pairs={{0,20},{4,16},{8,28},{12,24},{16,4},{20,0},{24,12},{28,8},{1,21},{... | collective-permute-start | bytes 1179656 | tf_op jit(solution)/shard_map/ppermute | solution.py:417
  62.5 48.3 %collective-permute-start.8 = (bf16[512,384]{1,0:T(8,128)(2,1)S(1)}, bf16[512,384]{1,0:T(8,128)(2,1)S(1)}, u32[]{:S(2)}, u32[]{:S(2)}) collective-permute-start(bf16[512,384]{1,0:T(8,128)(2,1)S(1)} %get-tuple-element.58), channel_id=1, source_target_pairs={{0,24},{4,28},{8,16},{12,20},{16,8},{20,12},{24,0},{28,4},{1,25},{... | collective-permute-start | bytes 1179656 | tf_op jit(solution)/shard_map/ppermute | solution.py:417
  80.6 30.3 %collective-permute-start.9 = (bf16[512,384]{1,0:T(8,128)(2,1)S(1)}, bf16[512,384]{1,0:T(8,128)(2,1)S(1)}, u32[]{:S(2)}, u32[]{:S(2)}) collective-permute-start(bf16[512,384]{1,0:T(8,128)(2,1)S(1)} %get-tuple-element.59), channel_id=1, source_target_pairs={{0,28},{4,24},{8,20},{12,16},{16,12},{20,8},{24,4},{28,0},{1,29},{... | collective-permute-start | bytes 1179656 | tf_op jit(solution)/shard_map/ppermute | solution.py:417
  151.5 24.7 %collective-permute-start.10 = (bf16[512,128]{1,0:T(8,128)(2,1)S(1)}, bf16[512,128]{1,0:T(8,128)(2,1)S(1)}, u32[]{:S(2)}, u32[]{:S(2)}) collective-permute-start(bf16[512,128]{1,0:T(8,128)(2,1)S(1)} %get-tuple-element.124), channel_id=1, source_target_pairs={{0,4},{4,0},{8,12},{12,8},{16,20},{20,16},{24,28},{28,24},{1,5},{5... | collective-permute-start | bytes 393224 | tf_op jit(solution)/shard_map/ppermute | solution.py:417
  152.1 26.6 %collective-permute-start.11 = (bf16[512,128]{1,0:T(8,128)(2,1)S(1)}, bf16[512,128]{1,0:T(8,128)(2,1)S(1)}, u32[]{:S(2)}, u32[]{:S(2)}) collective-permute-start(bf16[512,128]{1,0:T(8,128)(2,1)S(1)} %get-tuple-element.123), channel_id=1, source_target_pairs={{0,8},{4,12},{8,0},{12,4},{16,24},{20,28},{24,16},{28,20},{1,9},{5... | collective-permute-start | bytes 393224 | tf_op jit(solution)/shard_map/ppermute | solution.py:417
  168.8 18.2 %collective-permute-start.12 = (bf16[512,128]{1,0:T(8,128)(2,1)S(1)}, bf16[512,128]{1,0:T(8,128)(2,1)S(1)}, u32[]{:S(2)}, u32[]{:S(2)}) collective-permute-start(bf16[512,128]{1,0:T(8,128)(2,1)S(1)} %get-tuple-element.122), channel_id=1, source_target_pairs={{0,12},{4,8},{8,4},{12,0},{16,28},{20,24},{24,20},{28,16},{1,13},{... | collective-permute-start | bytes 393224 | tf_op jit(solution)/shard_map/ppermute | solution.py:417
  169.6 18.4 %collective-permute-start.13 = (bf16[512,128]{1,0:T(8,128)(2,1)S(1)}, bf16[512,128]{1,0:T(8,128)(2,1)S(1)}, u32[]{:S(2)}, u32[]{:S(2)}) collective-permute-start(bf16[512,128]{1,0:T(8,128)(2,1)S(1)} %get-tuple-element.121), channel_id=1, source_target_pairs={{0,16},{4,20},{8,24},{12,28},{16,0},{20,4},{24,8},{28,12},{1,17},{... | collective-permute-start | bytes 393224 | tf_op jit(solution)/shard_map/ppermute | solution.py:417
  173.5 17.3 %collective-permute-start.14 = (bf16[512,128]{1,0:T(8,128)(2,1)S(1)}, bf16[512,128]{1,0:T(8,128)(2,1)S(1)}, u32[]{:S(2)}, u32[]{:S(2)}) collective-permute-start(bf16[512,128]{1,0:T(8,128)(2,1)S(1)} %get-tuple-element.120), channel_id=1, source_target_pairs={{0,20},{4,16},{8,28},{12,24},{16,4},{20,0},{24,12},{28,8},{1,21},{... | collective-permute-start | bytes 393224 | tf_op jit(solution)/shard_map/ppermute | solution.py:417
  214.3 16.8 %collective-permute-start.17 = (bf16[512,128]{1,0:T(8,128)(2,1)S(1)}, bf16[512,128]{1,0:T(8,128)(2,1)S(1)}, u32[]{:S(2)}, u32[]{:S(2)}) collective-permute-start(bf16[512,128]{1,0:T(8,128)(2,1)S(1)} %get-tuple-element.63), channel_id=1, source_target_pairs={{0,4},{4,0},{8,12},{12,8},{16,20},{20,16},{24,28},{28,24},{1,5},{5... | collective-permute-start | bytes 393224 | tf_op jit(solution)/shard_map/ppermute | solution.py:417
  215.9 16.6 %collective-permute-start.18 = (bf16[512,128]{1,0:T(8,128)(2,1)S(1)}, bf16[512,128]{1,0:T(8,128)(2,1)S(1)}, u32[]{:S(2)}, u32[]{:S(2)}) collective-permute-start(bf16[512,128]{1,0:T(8,128)(2,1)S(1)} %get-tuple-element.64), channel_id=1, source_target_pairs={{0,8},{4,12},{8,0},{12,4},{16,24},{20,28},{24,16},{28,20},{1,9},{5... | collective-permute-start | bytes 393224 | tf_op jit(solution)/shard_map/ppermute | solution.py:417
  226.7 22.3 %collective-permute-start.25 = (bf16[2,192,3072]{2,1,0:T(8,128)(2,1)S(1)}, bf16[2,192,3072]{2,1,0:T(8,128)(2,1)S(1)}, u32[]{:S(2)}, u32[]{:S(2)}) collective-permute-start(bf16[2,192,3072]{2,1,0:T(8,128)(2,1)S(1)} %dynamic-slice_bitcast_fusion), channel_id=1, source_target_pairs={{0,1},{1,0},{2,3},{3,2},{4,5},{5,4},{6,7},{7,6},{8,9},{9,8},{10,11... | collective-permute-start | bytes 7077896 | tf_op jit(solution)/shard_map/ppermute | solution.py:461
  295.4 29.3 %collective-permute-start.28 = (bf16[512,384]{1,0:T(8,128)(2,1)S(1)}, bf16[512,384]{1,0:T(8,128)(2,1)S(1)}, u32[]{:S(2)}, u32[]{:S(2)}) collective-permute-start(bf16[512,384]{1,0:T(8,128)(2,1)S(1)} %get-tuple-element.80), channel_id=1, source_target_pairs={{0,8},{4,12},{8,0},{12,4},{16,24},{20,28},{24,16},{28,20},{1,9},{5... | collective-permute-start | bytes 1179656 | tf_op jit(solution)/shard_map/ppermute | solution.py:417
  300.5 37.8 %collective-permute-start.29 = (bf16[512,384]{1,0:T(8,128)(2,1)S(1)}, bf16[512,384]{1,0:T(8,128)(2,1)S(1)}, u32[]{:S(2)}, u32[]{:S(2)}) collective-permute-start(bf16[512,384]{1,0:T(8,128)(2,1)S(1)} %get-tuple-element.81), channel_id=1, source_target_pairs={{0,12},{4,8},{8,4},{12,0},{16,28},{20,24},{24,20},{28,16},{1,13},{... | collective-permute-start | bytes 1179656 | tf_op jit(solution)/shard_map/ppermute | solution.py:417
  300.5 40.2 %collective-permute-start.30 = (bf16[512,384]{1,0:T(8,128)(2,1)S(1)}, bf16[512,384]{1,0:T(8,128)(2,1)S(1)}, u32[]{:S(2)}, u32[]{:S(2)}) collective-permute-start(bf16[512,384]{1,0:T(8,128)(2,1)S(1)} %get-tuple-element.82), channel_id=1, source_target_pairs={{0,16},{4,20},{8,24},{12,28},{16,0},{20,4},{24,8},{28,12},{1,17},{... | collective-permute-start | bytes 1179656 | tf_op jit(solution)/shard_map/ppermute | solution.py:417
  303.3 53.2 %collective-permute-start.31 = (bf16[512,384]{1,0:T(8,128)(2,1)}, bf16[512,384]{1,0:T(8,128)(2,1)S(1)}, u32[]{:S(2)}, u32[]{:S(2)}) collective-permute-start(bf16[512,384]{1,0:T(8,128)(2,1)} %get-tuple-element.83), channel_id=1, source_target_pairs={{0,20},{4,16},{8,28},{12,24},{16,4},{20,0},{24,12},{28,8},{1,21},{... | collective-permute-start | bytes 1179656 | tf_op jit(solution)/shard_map/ppermute | solution.py:417
  304.9 52.3 %collective-permute-start.32 = (bf16[512,384]{1,0:T(8,128)(2,1)}, bf16[512,384]{1,0:T(8,128)(2,1)S(1)}, u32[]{:S(2)}, u32[]{:S(2)}) collective-permute-start(bf16[512,384]{1,0:T(8,128)(2,1)} %get-tuple-element.84), channel_id=1, source_target_pairs={{0,24},{4,28},{8,16},{12,20},{16,8},{20,12},{24,0},{28,4},{1,25},{... | collective-permute-start | bytes 1179656 | tf_op jit(solution)/shard_map/ppermute | solution.py:417
  324.8 33.2 %collective-permute-start.33 = (bf16[512,384]{1,0:T(8,128)(2,1)}, bf16[512,384]{1,0:T(8,128)(2,1)}, u32[]{:S(2)}, u32[]{:S(2)}) collective-permute-start(bf16[512,384]{1,0:T(8,128)(2,1)} %get-tuple-element.85), channel_id=1, source_target_pairs={{0,28},{4,24},{8,20},{12,16},{16,12},{20,8},{24,4},{28,0},{1,29},{... | collective-permute-start | bytes 1179656 | tf_op jit(solution)/shard_map/ppermute | solution.py:417
  339.1 45.5 %collective-permute-start.46 = (bf16[2,4,24,3840]{3,2,1,0:T(8,128)(2,1)}, bf16[2,4,24,3840]{3,2,1,0:T(8,128)(2,1)}, u32[]{:S(2)}, u32[]{:S(2)}) collective-permute-start(bf16[2,4,24,3840]{3,2,1,0:T(8,128)(2,1)} %get-tuple-element.106.refs_13_), channel_id=1, source_target_pairs={{0,4},{4,0},{8,12},{12,8},{16,20},{20,16},{24,28},{28,24},{1,5},{5... | collective-permute-start | bytes 4423688 | tf_op jit(solution)/shard_map/ppermute | solution.py:461
  341.5 40.7 %collective-permute-start.55 = (bf16[768,768]{1,0:T(8,128)(2,1)}, bf16[768,768]{1,0:T(8,128)(2,1)S(1)}, u32[]{:S(2)}, u32[]{:S(2)}) collective-permute-start(bf16[768,768]{1,0:T(8,128)(2,1)} %get-tuple-element.108.refs_12_), channel_id=1, source_target_pairs={{0,2},{1,3},{2,0},{3,1},{4,6},{5,7},{6,4},{7,5},{8,10},{9,11},{10,... | collective-permute-start | bytes 3538952 | tf_op jit(solution)/shard_map/ppermute | solution.py:461
  384.6 54.2 %collective-permute-start.34 = (bf16[2,192,2432]{2,1,0:T(8,128)(2,1)}, bf16[2,192,2432]{2,1,0:T(8,128)(2,1)}, u32[]{:S(2)}, u32[]{:S(2)}) collective-permute-start(bf16[2,192,2432]{2,1,0:T(8,128)(2,1)} %fusion.20), channel_id=1, source_target_pairs={{0,1},{1,0},{2,3},{3,2},{4,5},{5,4},{6,7},{7,6},{8,9},{9,8},{10,11... | collective-permute-start | bytes 5603336 | tf_op jit(solution)/shard_map/ppermute | solution.py:461
  394.8 21.0 %collective-permute-start.59 = (bf16[96,768]{1,0:T(8,128)(2,1)S(1)}, bf16[96,768]{1,0:T(8,128)(2,1)S(1)}, u32[]{:S(2)}, u32[]{:S(2)}) collective-permute-start(bf16[96,768]{1,0:T(8,128)(2,1)S(1)} %get-tuple-element.148), channel_id=1, source_target_pairs={{0,24},{4,28},{8,16},{12,20},{16,8},{20,12},{24,0},{28,4},{1,25},{... | collective-permute-start | bytes 442376 | tf_op jit(solution)/shard_map/ppermute | solution.py:461
  396.8 24.0 %collective-permute-start.58 = (bf16[96,768]{1,0:T(8,128)(2,1)S(1)}, bf16[96,768]{1,0:T(8,128)(2,1)S(1)}, u32[]{:S(2)}, u32[]{:S(2)}) collective-permute-start(bf16[96,768]{1,0:T(8,128)(2,1)S(1)} %get-tuple-element.149), channel_id=1, source_target_pairs={{0,16},{4,20},{8,24},{12,28},{16,0},{20,4},{24,8},{28,12},{1,17},{... | collective-permute-start | bytes 442376 | tf_op jit(solution)/shard_map/ppermute | solution.py:461
  412.5 21.7 %collective-permute-start.47 = (bf16[4,24,3840]{2,1,0:T(8,128)(2,1)S(1)}, bf16[4,24,3840]{2,1,0:T(8,128)(2,1)S(1)}, u32[]{:S(2)}, u32[]{:S(2)}) collective-permute-start(bf16[4,24,3840]{2,1,0:T(8,128)(2,1)S(1)} %get-tuple-element.112), channel_id=1, source_target_pairs={{0,2},{1,3},{2,0},{3,1},{4,6},{5,7},{6,4},{7,5},{8,10},{9,11},{10,... | collective-permute-start | bytes 2211848 | tf_op jit(solution)/shard_map/ppermute | solution.py:461
  433.4 44.8 %collective-permute-start.63 = (bf16[4,96,768]{2,1,0:T(8,128)(2,1)S(1)}, bf16[4,96,768]{2,1,0:T(8,128)(2,1)S(1)}, u32[]{:S(2)}, u32[]{:S(2)}) collective-permute-start(bf16[4,96,768]{2,1,0:T(8,128)(2,1)S(1)} %get-tuple-element.141), channel_id=1, source_target_pairs={{0,4},{4,0},{8,12},{12,8},{16,20},{20,16},{24,28},{28,24},{1,5},{5... | collective-permute-start | bytes 1769480 | tf_op jit(solution)/shard_map/ppermute | solution.py:461
  441.0 34.5 %collective-permute-start.37 = (bf16[2,4,24,1280]{3,2,1,0:T(8,128)(2,1)S(1)}, bf16[2,4,24,1280]{3,2,1,0:T(8,128)(2,1)S(1)}, u32[]{:S(2)}, u32[]{:S(2)}) collective-permute-start(bf16[2,4,24,1280]{3,2,1,0:T(8,128)(2,1)S(1)} %get-tuple-element.126), channel_id=1, source_target_pairs={{0,4},{4,0},{8,12},{12,8},{16,20},{20,16},{24,28},{28,24},{1,5},{5... | collective-permute-start | bytes 1474568 | tf_op jit(solution)/shard_map/ppermute | solution.py:461
  477.6 31.4 %collective-permute-start.54 = (bf16[4,24,3840]{2,1,0:T(8,128)(2,1)S(1)}, bf16[4,24,3840]{2,1,0:T(8,128)(2,1)S(1)}, u32[]{:S(2)}, u32[]{:S(2)}) collective-permute-start(bf16[4,24,3840]{2,1,0:T(8,128)(2,1)S(1)} %get-tuple-element.132), channel_id=1, source_target_pairs={{0,4},{4,0},{8,12},{12,8},{16,20},{20,16},{24,28},{28,24},{1,5},{5... | collective-permute-start | bytes 2211848 | tf_op jit(solution)/shard_map/ppermute | solution.py:461
  (96 other events, 979.0 us)
Sparse Core Ops, SparseCore 0:
  9.6 33.4 all-gather.6
  45.2 44.1 all-gather.10
  91.0 37.4 all-gather.8

commit v3 on v2

--- a/solution.py
+++ b/solution.py
@@ -73,10 +73,9 @@
     return [(at, size) for at in range(0, total, size)]
 
 
-def visible_pairs(key_meta_ref, query_meta_ref, block, at, size):
+def visible_pairs(key_meta_ref, query_meta_ref, block, span):
     key_place, key_doc = key_meta_ref[0, :, 0:1], key_meta_ref[0, :, 1:2]
-    query_place = query_meta_ref[block, 0:1, at : at + size]
-    query_doc = query_meta_ref[block, 1:2, at : at + size]
+    query_place, query_doc = query_meta_ref[block, 0:1, span], query_meta_ref[block, 1:2, span]
     return (key_place <= query_place) & (key_doc == query_doc)
 
 
@@ -100,22 +99,28 @@
 
     def work(block, partial):
         keys, values = k_ref[0], v_ref[0]
-        for at, size in column_chunks(total):
-            span = slice(at, at + size)
-            s = dot_nt(keys, rows_ref[block, span, :])
+        spans = [slice(at, at + size) for at, size in column_chunks(total)]
+        old_max = [max_ref[block, :, span] for span in spans]
+        old_sum = [sum_ref[block, :, span] for span in spans]
+        old_out = [out_ref[block, :, span] for span in spans]
+        scores = [dot_nt(keys, rows_ref[block, span, :]) for span in spans]
+        done = []
+        for i, s in enumerate(scores):
             if partial:
-                visible = visible_pairs(key_meta_ref, query_meta_ref, block, at, size)
+                visible = visible_pairs(key_meta_ref, query_meta_ref, block, spans[i])
                 s = jnp.where(visible, s, NEG)
-            old_max = max_ref[block, :, span]
-            new_max = jnp.maximum(old_max, jnp.max(s, 0, keepdims=True))
+            new_max = jnp.maximum(old_max[i], jnp.max(s, 0, keepdims=True))
             weights = jnp.exp(s - new_max)
             if partial:
                 weights = jnp.where(visible, weights, 0.0)
-            factor = jnp.exp(old_max - new_max)
+            factor = jnp.exp(old_max[i] - new_max)
+            new_sum = old_sum[i] * factor + jnp.sum(weights, 0, keepdims=True)
+            added = dot_tn(values, weights.astype(jnp.bfloat16))
+            done.append((new_max, new_sum, old_out[i] * factor + added))
+        for span, (new_max, new_sum, new_out) in zip(spans, done):
             max_ref[block, :, span] = new_max
-            sum_ref[block, :, span] = sum_ref[block, :, span] * factor + jnp.sum(weights, 0, keepdims=True)
-            added = dot_tn(values, weights.astype(jnp.bfloat16))
-            out_ref[block, :, span] = out_ref[block, :, span] * factor + added
+            sum_ref[block, :, span] = new_sum
+            out_ref[block, :, span] = new_out
 
     @pl.loop(0, blocks)
     def _(block):
@@ -171,8 +176,7 @@
             grad_rows = grad_rows_ref[block, span, :]
             prob = jnp.exp(dot_nt(keys, q_rows) - log_ref[block, :, span])
             if partial:
-                visible = visible_pairs(key_meta_ref, query_meta_ref, block, at, size)
-                prob = jnp.where(visible, prob, 0.0)
+                prob = jnp.where(visible_pairs(key_meta_ref, query_meta_ref, block, span), prob, 0.0)
             grad_prob = dot_nt(values, grad_rows)
             sum_v_ref[...] += dot_nn(prob.astype(bf16), grad_rows)
             grad_score = (prob * (grad_prob - delta_ref[block, :, span])).astype(bf16)
@@ -311,6 +315,11 @@
     width = 128
     parts = windows_ref.shape[2] // width
     per_part = rows_ref.shape[1] // parts
+
+    @pl.when(pl.program_id(0) == 0)
+    def _():
+        sums_ref[...] = jnp.zeros_like(sums_ref)
+
     for k, value_ref in enumerate(ins):
         windows_ref[jnp.bitwise_xor(me_ref[0], k)] = value_ref[...]
     for i in range(parts):
@@ -328,7 +337,7 @@
                 at = i * per_part + (3 * t + m) * width
                 value = value.astype(rows_ref.dtype)
                 rows_ref[:, at : at + width] = value
-                sums_ref[:, at : at + width] = jnp.sum(value.astype(f32), 0, keepdims=True)
+                sums_ref[:, at : at + width] += jnp.sum(value.astype(f32), 0, keepdims=True)
 
 
 SMEM_SPEC = pl.BlockSpec(memory_space=pltpu.SMEM)
@@ -396,15 +405,19 @@
 def join_rows(me, pieces, model_width, earlier=()):
     count, columns = pieces[0].shape
     total = model_width * columns // 128
+    step = count // 4
     return pl.pallas_call(
         leading(join_kernel, 1 + HEAD_GROUPS, len(earlier)),
-        in_specs=[SMEM_SPEC] + [VMEM_SPEC] * HEAD_GROUPS + [ANY_SPEC] * len(earlier),
-        out_specs=[VMEM_SPEC, VMEM_SPEC],
+        grid=(count // step,),
+        in_specs=[SMEM_SPEC]
+        + [pl.BlockSpec((step, columns), lambda i: (i, 0))] * HEAD_GROUPS
+        + [ANY_SPEC] * len(earlier),
+        out_specs=[pl.BlockSpec((step, total), lambda i: (i, 0)), pl.BlockSpec((1, total), lambda i: (0, 0))],
         out_shape=[
             jax.ShapeDtypeStruct((count, total), pieces[0].dtype),
             jax.ShapeDtypeStruct((1, total), jnp.float32),
         ],
-        scratch_shapes=[pltpu.VMEM((HEAD_GROUPS, count, columns), pieces[0].dtype)],
+        scratch_shapes=[pltpu.VMEM((HEAD_GROUPS, step, columns), pieces[0].dtype)],
         compiler_params=LOCAL,
         cost_estimate=pl.CostEstimate(flops=0, bytes_accessed=4 * count * total * 2, transcendentals=0),
         name="join_rows",

time: 534 us -> 515 us (0.964)
  Pallas kernels: 83.1 us -> 65.1 us
    pallas_call x1, Pallas kernels: 37.4 us -> 24.1 us  [per_device(): out_windows, out_columns, log_total = forward_call(*operands)]
    pallas_call x1, Pallas kernels: 33.9 us -> 28.4 us  [per_device(): backward_call(*operands, taken_grad, out_columns, log_total, *earlier)]
  transfers between devices with their start and end apart: 67 -> 67, of which waited for: 29 -> 28; matrix products, arithmetic and copies ran while one was open for 14% -> 15% of each run, Pallas kernels for 9% -> 6%
where the time goes in v3:
time: 515 us; the launch traced here: 508 us
  waiting for transfers between devices  170 us (33%)
  starting transfers between devices  136 us (26%)
  Pallas kernels  65.1 us (13%)
  matrix products  53.8 us (10%)
  local copies, waits for them, and re-layouts  45.9 us (9%)
  other arithmetic  17.3 us (3%)
  between operations  15.2 us (3%)
  blocking collectives  5.2 us (1%)
    ppermute x28, waiting for transfers between devices, swapped(): lax.ppermute(pieces[k], axis, [(i, i ^ k) for i in range(length)])  90.8 us
    ppermute x36, starting transfers between devices, exchange(): lax.ppermute(value, axis, [(i, i ^ by) for i in range(lax.axis_size(axis))])  70.4 us
    ppermute x28, starting transfers between devices, swapped(): lax.ppermute(pieces[k], axis, [(i, i ^ k) for i in range(length)])  65 us
    ppermute x36, waiting for transfers between devices, exchange(): lax.ppermute(value, axis, [(i, i ^ by) for i in range(lax.axis_size(axis))])  64.1 us
    pallas_call x1, Pallas kernels, per_device(): backward_call(*operands, taken_grad, out_columns, log_total, *earlier)  28.4 us
    pallas_call x1, Pallas kernels, per_device(): out_windows, out_columns, log_total = forward_call(*operands)  24.1 us
    unnamed x142, local copies, waits for them, and re-layouts  17.9 us
    all_gather x1, waiting for transfers between devices, per_device(): wqkv_all = lax.all_gather(w_qkv, 'fsdp', axis=0, tiled=True)  14.2 us
  transfers between devices with their start and end apart: 67, of which 28 were waited for; matrix products, arithmetic and copies ran while one was open for 15% of the time, Pallas kernels for 6%

profile of v3, /device:TPU:0, one launch (start us, length us, event | category | flops | bytes accessed | tf_op | source)
XLA Modules:
  0.0 508.0 jit_solution(5738641771656202377)
XLA Ops:
  14.1 5.2 %all-gather.2 = bf16[4,1,2304]{2,1,0:T(2,128)(2,1)S(1)} all-gather(bf16[1,1,2304]{2,1,0:T(2,128)(2,1)S(1)} %reshape.270), channel_id=2, replica_groups=mesh['ctx'=8,'fsdp'=4] {'fsdp'}, dimensions={0}, use_global_device_ids=true | all-gather | bytes 23040 | tf_op jit(solution)/shard_map/all_gather | solution.py:538
  28.9 14.2 %all-gather.7.cloned.1.call-done = bf16[768,2304]{1,0:T(8,128)(2,1)} async-done(((bf16[192,2304]{1,0:T(8,128)(2,1)}), bf16[768,2304]{1,0:T(8,128)(2,1)}) %all-gather.7.cloned.1.call-update) | async-done | bytes 3538960 | tf_op jit(solution)/shard_map/all_gather | solution.py:543
  43.1 4.2 fusion.9.rows_ref
  65.9 14.6 %collective-permute-done.4 = bf16[512,384]{1,0:T(8,128)(2,1)S(1)} collective-permute-done((bf16[512,384]{1,0:T(8,128)(2,1)S(1)}, bf16[512,384]{1,0:T(8,128)(2,1)S(1)}, u32[]{:S(2)}, u32[]{:S(2)}) %collective-permute-start.4) | collective-permute-done | bytes 393248 | tf_op jit(solution)/shard_map/ppermute | solution.py:430
  81.7 5.8 %collective-permute-done.5 = bf16[512,384]{1,0:T(8,128)(2,1)S(1)} collective-permute-done((bf16[512,384]{1,0:T(8,128)(2,1)S(1)}, bf16[512,384]{1,0:T(8,128)(2,1)S(1)}, u32[]{:S(2)}, u32[]{:S(2)}) %collective-permute-start.5) | collective-permute-done | bytes 393248 | tf_op jit(solution)/shard_map/ppermute | solution.py:430
  87.7 23.1 %collective-permute-done.7 = bf16[512,384]{1,0:T(8,128)(2,1)S(1)} collective-permute-done((bf16[512,384]{1,0:T(8,128)(2,1)S(1)}, bf16[512,384]{1,0:T(8,128)(2,1)S(1)}, u32[]{:S(2)}, u32[]{:S(2)}) %collective-permute-start.7) | collective-permute-done | bytes 393248 | tf_op jit(solution)/shard_map/ppermute | solution.py:430
  112.7 24.1 %attend.1 = (bf16[8,512,128]{2,1,0:T(8,128)(2,1)}, f32[8,128,768]{2,1,0:T(8,128)}, f32[8,1,768]{2,1,0:T(1,128)}) custom-call(s32[64]{0:T(128)} %reshape.256.kind_ref.refs_0_, s32[1]{0:T(128)} %bitcast.3.side_ref.refs_1_, bf16[8,512,384]{2,1,0:T(8,128)(2,1)} %copy-done.30, bf16[8,512,384]{2,1,0:T(8,128)(2,1)} %copy-done.30, bf16[8,512,384]{2,1,0:T(8,128)(2,1)} %copy-done.30, ...), custom_call_target="tpu_custom_call" | custom-call | flops 28991029248 | bytes 16777216 | tf_op jit(solution)/shard_map/attend/pallas_call | solution.py:569
  138.8 15.7 %collective-permute-start.11 = (bf16[512,128]{1,0:T(8,128)(2,1)S(1)}, bf16[512,128]{1,0:T(8,128)(2,1)S(1)}, u32[]{:S(2)}, u32[]{:S(2)}) collective-permute-start(bf16[512,128]{1,0:T(8,128)(2,1)S(1)} %get-tuple-element.123), channel_id=1, source_target_pairs={{0,8},{4,12},{8,0},{12,4},{16,24},{20,28},{24,16},{28,20},{1,9},{5... | collective-permute-start | bytes 393224 | tf_op jit(solution)/shard_map/ppermute | solution.py:430
  156.3 3.9 collective-permute-start.13
  167.7 4.6 convolution_bitcast_fusion.refs_11_
  181.6 12.8 %fusion.73 = (bf16[3072]{0:T(1024)(128)(2,1)}, bf16[512,3072]{1,0:T(8,128)(2,1)S(1)}, f32[512,3072]{1,0:T(8,128)}) fusion(f32[512,3072]{1,0:T(8,128)} %convolution_bitcast_fusion.refs_11_, f32[3072]{0:T(1024)S(1)} %copy-done.37, bf16[512,768]{1,0:T(8,128)(2,1)S(1)} %add_convert_fusion.1.refs_1_, bf16[768,3072]{1,0:T(8,128)(2,1)} %all-gather.9.cloned.1.call-done), kind=kOutput, calls=%fused_computation.228 | convolution fusion | flops 2450519040 | bytes 21252096 | tf_op jit(solution)/shard_map/dot_general | solution.py:580
  194.5 3.6 multiply_reduce_fusion
  203.3 4.4 collective-permute-start.18
  214.2 4.2 convolution_convert_fusion.2
  224.6 9.6 %collective-permute-done.21 = bf16[512,128]{1,0:T(8,128)(2,1)S(1)} collective-permute-done((bf16[512,128]{1,0:T(8,128)(2,1)S(1)}, bf16[512,128]{1,0:T(8,128)(2,1)S(1)}, u32[]{:S(2)}, u32[]{:S(2)}) %collective-permute-start.21) | collective-permute-done | bytes 131104 | tf_op jit(solution)/shard_map/ppermute | solution.py:430
  241.7 28.4 %attend_back.1 = (bf16[8,512,128]{2,1,0:T(8,128)(2,1)}, bf16[8,512,128]{2,1,0:T(8,128)(2,1)}, bf16[8,512,128]{2,1,0:T(8,128)(2,1)}) custom-call(s32[64]{0:T(128)} %reshape.256.kind_ref.refs_0_, s32[1]{0:T(128)} %bitcast.3.side_ref.refs_1_, bf16[8,512,384]{2,1,0:T(8,128)(2,1)} %copy-done.30, bf16[8,512,384]{2,1,0:T(8,128)(2,1)} %copy-done.30, ...), custom_call_target="tpu_custom_call" | custom-call | flops 72477573120 | bytes 25165824 | tf_op jit(solution)/shard_map/attend_back/pallas_call | solution.py:664
  277.3 4.1 collective-permute-start.28
  289.4 17.4 %collective-permute-done.28.refs_3_ = bf16[512,384]{1,0:T(8,128)(2,1)S(1)} collective-permute-done((bf16[512,384]{1,0:T(8,128)(2,1)S(1)}, bf16[512,384]{1,0:T(8,128)(2,1)S(1)}, u32[]{:S(2)}, u32[]{:S(2)}) %collective-permute-start.28) | collective-permute-done | bytes 393248 | tf_op jit(solution)/shard_map/ppermute | solution.py:430
  308.2 9.4 %fusion.33 = bf16[1,512,768]{2,1,0:T(8,128)(2,1)} fusion(f32[512,768]{1,0:T(8,128)} %copy-done.24, bf16[3072,768]{1,0:T(8,128)(2,1)} %bitcast.302, f32[768]{0:T(1024)S(1)} %add.273, f32[512,3072]{1,0:T(8,128)} %get-tuple-element.181, f32[3072]{0:T(1024)S(1)} %copy-done.38), kind=kOutput, calls=%fused_computation.77 | convolution fusion | flops 2432827392 | bytes 13384704 | tf_op jit(solution)/shard_map/dot_general | solution.py:583
  326.4 12.0 %collective-permute-done.31.refs_6_ = bf16[512,384]{1,0:T(8,128)(2,1)S(1)} collective-permute-done((bf16[512,384]{1,0:T(8,128)(2,1)}, bf16[512,384]{1,0:T(8,128)(2,1)S(1)}, u32[]{:S(2)}, u32[]{:S(2)}) %collective-permute-start.31) | collective-permute-done | bytes 393248 | tf_op jit(solution)/shard_map/ppermute | solution.py:430
  350.1 6.2 %fusion.30 = (bf16[768]{0:T(1024)(128)(2,1)}, f32[512]{0:T(512)}, f32[512]{0:T(512)}, bf16[768]{0:T(1024)(128)(2,1)}, f32[512,768]{1,0:T(8,128)}) fusion(bf16[1,512,768]{2,1,0:T(8,128)(2,1)} %param.16, f32[512]{0:T(512)} %copy-done.39, f32[512]{0:T(512)S(1)} %copy-done.32, f32[768]{0:T(1024)} %copy-done.35, ...), kind=kOutput, calls=%fused_computation.54 | convolution fusion | flops 1815868928 | bytes 8271872 | tf_op jit(solution)/shard_map/te,de->td/dot_general | solution.py:680
  369.7 8.0 %collective-permute-done.56.refs_1_ = bf16[4,96,768]{2,1,0:T(8,128)(2,1)S(1)} collective-permute-done((bf16[4,96,768]{2,1,0:T(8,128)(2,1)S(1)}, bf16[4,96,768]{2,1,0:T(8,128)(2,1)S(1)}, u32[]{:S(2)}, u32[]{:S(2)}) %collective-permute-start.56) | collective-permute-done | bytes 589856 | tf_op jit(solution)/shard_map/ppermute | solution.py:474
  380.0 15.5 %collective-permute-start.58 = (bf16[96,768]{1,0:T(8,128)(2,1)S(1)}, bf16[96,768]{1,0:T(8,128)(2,1)S(1)}, u32[]{:S(2)}, u32[]{:S(2)}) collective-permute-start(bf16[96,768]{1,0:T(8,128)(2,1)S(1)} %get-tuple-element.149), channel_id=1, source_target_pairs={{0,16},{4,20},{8,24},{12,28},{16,0},{20,4},{24,8},{28,12},{1,17},{... | collective-permute-start | bytes 442376 | tf_op jit(solution)/shard_map/ppermute | solution.py:474
  399.0 4.5 collective-permute-done.58
  412.1 4.7 collective-permute-done.61
  426.8 7.2 %collective-permute-done.49 = bf16[24,3840]{1,0:T(8,128)(2,1)S(1)} collective-permute-done((bf16[24,3840]{1,0:T(8,128)(2,1)S(1)}, bf16[24,3840]{1,0:T(8,128)(2,1)S(1)}, u32[]{:S(2)}, u32[]{:S(2)}) %collective-permute-start.49) | collective-permute-done | bytes 184352 | tf_op jit(solution)/shard_map/ppermute | solution.py:474
  438.6 5.0 collective-permute-done.53
  443.5 4.0 collective-permute-start.35
  450.0 3.8 collective-permute-done.35.refs_1_
  465.0 5.2 %collective-permute-start.40 = (bf16[24,2432]{1,0:T(8,128)(2,1)S(1)}, bf16[24,2432]{1,0:T(8,128)(2,1)S(1)}, u32[]{:S(2)}, u32[]{:S(2)}) collective-permute-start(bf16[24,2432]{1,0:T(8,128)(2,1)S(1)} %get-tuple-element.159), channel_id=1, source_target_pairs={{0,16},{4,20},{8,24},{12,28},{16,0},{20,4},{24,8},{28,12},{1,17},{... | collective-permute-start | bytes 350216 | tf_op jit(solution)/shard_map/ppermute | solution.py:474
  470.3 8.9 %collective-permute-done.40 = bf16[24,2432]{1,0:T(8,128)(2,1)S(1)} collective-permute-done((bf16[24,2432]{1,0:T(8,128)(2,1)S(1)}, bf16[24,2432]{1,0:T(8,128)(2,1)S(1)}, u32[]{:S(2)}, u32[]{:S(2)}) %collective-permute-start.40) | collective-permute-done | bytes 116768 | tf_op jit(solution)/shard_map/ppermute | solution.py:474
  493.1 4.3 collective-permute-done.45
  (386 shorter events, 194.4 us)
Async XLA Ops:
  7.2 35.9 %all-gather.7.cloned.1.call-start = ((), (), s32[]{:S(2)}) async-start(), calls=%async_computation | async-start | bytes 4423680 | tf_op jit(solution)/shard_map/all_gather | solution.py:543
  8.0 152.2 %all-gather.11.cloned.1.call-start = ((), (), s32[]{:S(2)}) async-start(), calls=%async_computation.2 | async-start | bytes 7372800 | tf_op jit(solution)/shard_map/all_gather | solution.py:545
  10.8 170.8 %all-gather.9.cloned.1.call-start = ((), (), s32[]{:S(2)}) async-start(), calls=%async_computation.1 | async-start | bytes 5898240 | tf_op jit(solution)/shard_map/all_gather | solution.py:544
  52.8 27.8 %collective-permute-start.4 = (bf16[512,384]{1,0:T(8,128)(2,1)S(1)}, bf16[512,384]{1,0:T(8,128)(2,1)S(1)}, u32[]{:S(2)}, u32[]{:S(2)}) collective-permute-start(bf16[512,384]{1,0:T(8,128)(2,1)S(1)} %get-tuple-element.54), channel_id=1, source_target_pairs={{0,8},{4,12},{8,0},{12,4},{16,24},{20,28},{24,16},{28,20},{1,9},{5... | collective-permute-start | bytes 1179656 | tf_op jit(solution)/shard_map/ppermute | solution.py:430
  54.2 33.3 %collective-permute-start.5 = (bf16[512,384]{1,0:T(8,128)(2,1)S(1)}, bf16[512,384]{1,0:T(8,128)(2,1)S(1)}, u32[]{:S(2)}, u32[]{:S(2)}) collective-permute-start(bf16[512,384]{1,0:T(8,128)(2,1)S(1)} %get-tuple-element.55), channel_id=1, source_target_pairs={{0,12},{4,8},{8,4},{12,0},{16,28},{20,24},{24,20},{28,16},{1,13},{... | collective-permute-start | bytes 1179656 | tf_op jit(solution)/shard_map/ppermute | solution.py:430
  54.8 32.8 %collective-permute-start.6 = (bf16[512,384]{1,0:T(8,128)(2,1)S(1)}, bf16[512,384]{1,0:T(8,128)(2,1)S(1)}, u32[]{:S(2)}, u32[]{:S(2)}) collective-permute-start(bf16[512,384]{1,0:T(8,128)(2,1)S(1)} %get-tuple-element.56), channel_id=1, source_target_pairs={{0,16},{4,20},{8,24},{12,28},{16,0},{20,4},{24,8},{28,12},{1,17},{... | collective-permute-start | bytes 1179656 | tf_op jit(solution)/shard_map/ppermute | solution.py:430
  57.2 53.6 %collective-permute-start.7 = (bf16[512,384]{1,0:T(8,128)(2,1)S(1)}, bf16[512,384]{1,0:T(8,128)(2,1)S(1)}, u32[]{:S(2)}, u32[]{:S(2)}) collective-permute-start(bf16[512,384]{1,0:T(8,128)(2,1)S(1)} %get-tuple-element.57), channel_id=1, source_target_pairs={{0,20},{4,16},{8,28},{12,24},{16,4},{20,0},{24,12},{28,8},{1,21},{... | collective-permute-start | bytes 1179656 | tf_op jit(solution)/shard_map/ppermute | solution.py:430
  62.5 48.3 %collective-permute-start.8 = (bf16[512,384]{1,0:T(8,128)(2,1)S(1)}, bf16[512,384]{1,0:T(8,128)(2,1)S(1)}, u32[]{:S(2)}, u32[]{:S(2)}) collective-permute-start(bf16[512,384]{1,0:T(8,128)(2,1)S(1)} %get-tuple-element.58), channel_id=1, source_target_pairs={{0,24},{4,28},{8,16},{12,20},{16,8},{20,12},{24,0},{28,4},{1,25},{... | collective-permute-start | bytes 1179656 | tf_op jit(solution)/shard_map/ppermute | solution.py:430
  80.6 30.3 %collective-permute-start.9 = (bf16[512,384]{1,0:T(8,128)(2,1)S(1)}, bf16[512,384]{1,0:T(8,128)(2,1)S(1)}, u32[]{:S(2)}, u32[]{:S(2)}) collective-permute-start(bf16[512,384]{1,0:T(8,128)(2,1)S(1)} %get-tuple-element.59), channel_id=1, source_target_pairs={{0,28},{4,24},{8,20},{12,16},{16,12},{20,8},{24,4},{28,0},{1,29},{... | collective-permute-start | bytes 1179656 | tf_op jit(solution)/shard_map/ppermute | solution.py:430
  138.2 24.7 %collective-permute-start.10 = (bf16[512,128]{1,0:T(8,128)(2,1)S(1)}, bf16[512,128]{1,0:T(8,128)(2,1)S(1)}, u32[]{:S(2)}, u32[]{:S(2)}) collective-permute-start(bf16[512,128]{1,0:T(8,128)(2,1)S(1)} %get-tuple-element.124), channel_id=1, source_target_pairs={{0,4},{4,0},{8,12},{12,8},{16,20},{20,16},{24,28},{28,24},{1,5},{5... | collective-permute-start | bytes 393224 | tf_op jit(solution)/shard_map/ppermute | solution.py:430
  138.8 26.6 %collective-permute-start.11 = (bf16[512,128]{1,0:T(8,128)(2,1)S(1)}, bf16[512,128]{1,0:T(8,128)(2,1)S(1)}, u32[]{:S(2)}, u32[]{:S(2)}) collective-permute-start(bf16[512,128]{1,0:T(8,128)(2,1)S(1)} %get-tuple-element.123), channel_id=1, source_target_pairs={{0,8},{4,12},{8,0},{12,4},{16,24},{20,28},{24,16},{28,20},{1,9},{5... | collective-permute-start | bytes 393224 | tf_op jit(solution)/shard_map/ppermute | solution.py:430
  155.5 18.2 %collective-permute-start.12 = (bf16[512,128]{1,0:T(8,128)(2,1)S(1)}, bf16[512,128]{1,0:T(8,128)(2,1)S(1)}, u32[]{:S(2)}, u32[]{:S(2)}) collective-permute-start(bf16[512,128]{1,0:T(8,128)(2,1)S(1)} %get-tuple-element.122), channel_id=1, source_target_pairs={{0,12},{4,8},{8,4},{12,0},{16,28},{20,24},{24,20},{28,16},{1,13},{... | collective-permute-start | bytes 393224 | tf_op jit(solution)/shard_map/ppermute | solution.py:430
  156.3 18.8 %collective-permute-start.13 = (bf16[512,128]{1,0:T(8,128)(2,1)S(1)}, bf16[512,128]{1,0:T(8,128)(2,1)S(1)}, u32[]{:S(2)}, u32[]{:S(2)}) collective-permute-start(bf16[512,128]{1,0:T(8,128)(2,1)S(1)} %get-tuple-element.121), channel_id=1, source_target_pairs={{0,16},{4,20},{8,24},{12,28},{16,0},{20,4},{24,8},{28,12},{1,17},{... | collective-permute-start | bytes 393224 | tf_op jit(solution)/shard_map/ppermute | solution.py:430
  160.2 17.6 %collective-permute-start.14 = (bf16[512,128]{1,0:T(8,128)(2,1)S(1)}, bf16[512,128]{1,0:T(8,128)(2,1)S(1)}, u32[]{:S(2)}, u32[]{:S(2)}) collective-permute-start(bf16[512,128]{1,0:T(8,128)(2,1)S(1)} %get-tuple-element.120), channel_id=1, source_target_pairs={{0,20},{4,16},{8,28},{12,24},{16,4},{20,0},{24,12},{28,8},{1,21},{... | collective-permute-start | bytes 393224 | tf_op jit(solution)/shard_map/ppermute | solution.py:430
  201.7 16.9 %collective-permute-start.17 = (bf16[512,128]{1,0:T(8,128)(2,1)S(1)}, bf16[512,128]{1,0:T(8,128)(2,1)S(1)}, u32[]{:S(2)}, u32[]{:S(2)}) collective-permute-start(bf16[512,128]{1,0:T(8,128)(2,1)S(1)} %get-tuple-element.63), channel_id=1, source_target_pairs={{0,4},{4,0},{8,12},{12,8},{16,20},{20,16},{24,28},{28,24},{1,5},{5... | collective-permute-start | bytes 393224 | tf_op jit(solution)/shard_map/ppermute | solution.py:430
  203.3 16.8 %collective-permute-start.18 = (bf16[512,128]{1,0:T(8,128)(2,1)S(1)}, bf16[512,128]{1,0:T(8,128)(2,1)S(1)}, u32[]{:S(2)}, u32[]{:S(2)}) collective-permute-start(bf16[512,128]{1,0:T(8,128)(2,1)S(1)} %get-tuple-element.64), channel_id=1, source_target_pairs={{0,8},{4,12},{8,0},{12,4},{16,24},{20,28},{24,16},{28,20},{1,9},{5... | collective-permute-start | bytes 393224 | tf_op jit(solution)/shard_map/ppermute | solution.py:430
  214.1 22.3 %collective-permute-start.25 = (bf16[2,192,3072]{2,1,0:T(8,128)(2,1)S(1)}, bf16[2,192,3072]{2,1,0:T(8,128)(2,1)S(1)}, u32[]{:S(2)}, u32[]{:S(2)}) collective-permute-start(bf16[2,192,3072]{2,1,0:T(8,128)(2,1)S(1)} %dynamic-slice_bitcast_fusion), channel_id=1, source_target_pairs={{0,1},{1,0},{2,3},{3,2},{4,5},{5,4},{6,7},{7,6},{8,9},{9,8},{10,11... | collective-permute-start | bytes 7077896 | tf_op jit(solution)/shard_map/ppermute | solution.py:474
  277.3 29.4 %collective-permute-start.28 = (bf16[512,384]{1,0:T(8,128)(2,1)S(1)}, bf16[512,384]{1,0:T(8,128)(2,1)S(1)}, u32[]{:S(2)}, u32[]{:S(2)}) collective-permute-start(bf16[512,384]{1,0:T(8,128)(2,1)S(1)} %get-tuple-element.80), channel_id=1, source_target_pairs={{0,8},{4,12},{8,0},{12,4},{16,24},{20,28},{24,16},{28,20},{1,9},{5... | collective-permute-start | bytes 1179656 | tf_op jit(solution)/shard_map/ppermute | solution.py:430
  282.4 37.8 %collective-permute-start.29 = (bf16[512,384]{1,0:T(8,128)(2,1)S(1)}, bf16[512,384]{1,0:T(8,128)(2,1)S(1)}, u32[]{:S(2)}, u32[]{:S(2)}) collective-permute-start(bf16[512,384]{1,0:T(8,128)(2,1)S(1)} %get-tuple-element.81), channel_id=1, source_target_pairs={{0,12},{4,8},{8,4},{12,0},{16,28},{20,24},{24,20},{28,16},{1,13},{... | collective-permute-start | bytes 1179656 | tf_op jit(solution)/shard_map/ppermute | solution.py:430
  282.4 40.1 %collective-permute-start.30 = (bf16[512,384]{1,0:T(8,128)(2,1)S(1)}, bf16[512,384]{1,0:T(8,128)(2,1)S(1)}, u32[]{:S(2)}, u32[]{:S(2)}) collective-permute-start(bf16[512,384]{1,0:T(8,128)(2,1)S(1)} %get-tuple-element.82), channel_id=1, source_target_pairs={{0,16},{4,20},{8,24},{12,28},{16,0},{20,4},{24,8},{28,12},{1,17},{... | collective-permute-start | bytes 1179656 | tf_op jit(solution)/shard_map/ppermute | solution.py:430
  285.3 53.1 %collective-permute-start.31 = (bf16[512,384]{1,0:T(8,128)(2,1)}, bf16[512,384]{1,0:T(8,128)(2,1)S(1)}, u32[]{:S(2)}, u32[]{:S(2)}) collective-permute-start(bf16[512,384]{1,0:T(8,128)(2,1)} %get-tuple-element.83), channel_id=1, source_target_pairs={{0,20},{4,16},{8,28},{12,24},{16,4},{20,0},{24,12},{28,8},{1,21},{... | collective-permute-start | bytes 1179656 | tf_op jit(solution)/shard_map/ppermute | solution.py:430
  287.0 52.1 %collective-permute-start.32 = (bf16[512,384]{1,0:T(8,128)(2,1)}, bf16[512,384]{1,0:T(8,128)(2,1)S(1)}, u32[]{:S(2)}, u32[]{:S(2)}) collective-permute-start(bf16[512,384]{1,0:T(8,128)(2,1)} %get-tuple-element.84), channel_id=1, source_target_pairs={{0,24},{4,28},{8,16},{12,20},{16,8},{20,12},{24,0},{28,4},{1,25},{... | collective-permute-start | bytes 1179656 | tf_op jit(solution)/shard_map/ppermute | solution.py:430
  306.8 33.1 %collective-permute-start.33 = (bf16[512,384]{1,0:T(8,128)(2,1)}, bf16[512,384]{1,0:T(8,128)(2,1)}, u32[]{:S(2)}, u32[]{:S(2)}) collective-permute-start(bf16[512,384]{1,0:T(8,128)(2,1)} %get-tuple-element.85), channel_id=1, source_target_pairs={{0,28},{4,24},{8,20},{12,16},{16,12},{20,8},{24,4},{28,0},{1,29},{... | collective-permute-start | bytes 1179656 | tf_op jit(solution)/shard_map/ppermute | solution.py:430
  321.0 46.3 %collective-permute-start.46 = (bf16[2,4,24,3840]{3,2,1,0:T(8,128)(2,1)}, bf16[2,4,24,3840]{3,2,1,0:T(8,128)(2,1)}, u32[]{:S(2)}, u32[]{:S(2)}) collective-permute-start(bf16[2,4,24,3840]{3,2,1,0:T(8,128)(2,1)} %get-tuple-element.106.refs_13_), channel_id=1, source_target_pairs={{0,4},{4,0},{8,12},{12,8},{16,20},{20,16},{24,28},{28,24},{1,5},{5... | collective-permute-start | bytes 4423688 | tf_op jit(solution)/shard_map/ppermute | solution.py:474
  323.4 41.5 %collective-permute-start.55 = (bf16[768,768]{1,0:T(8,128)(2,1)}, bf16[768,768]{1,0:T(8,128)(2,1)S(1)}, u32[]{:S(2)}, u32[]{:S(2)}) collective-permute-start(bf16[768,768]{1,0:T(8,128)(2,1)} %get-tuple-element.108.refs_12_), channel_id=1, source_target_pairs={{0,2},{1,3},{2,0},{3,1},{4,6},{5,7},{6,4},{7,5},{8,10},{9,11},{10,... | collective-permute-start | bytes 3538952 | tf_op jit(solution)/shard_map/ppermute | solution.py:474
  367.3 54.5 %collective-permute-start.34 = (bf16[2,192,2432]{2,1,0:T(8,128)(2,1)}, bf16[2,192,2432]{2,1,0:T(8,128)(2,1)}, u32[]{:S(2)}, u32[]{:S(2)}) collective-permute-start(bf16[2,192,2432]{2,1,0:T(8,128)(2,1)} %fusion.20), channel_id=1, source_target_pairs={{0,1},{1,0},{2,3},{3,2},{4,5},{5,4},{6,7},{7,6},{8,9},{9,8},{10,11... | collective-permute-start | bytes 5603336 | tf_op jit(solution)/shard_map/ppermute | solution.py:474
  377.9 21.1 %collective-permute-start.59 = (bf16[96,768]{1,0:T(8,128)(2,1)S(1)}, bf16[96,768]{1,0:T(8,128)(2,1)S(1)}, u32[]{:S(2)}, u32[]{:S(2)}) collective-permute-start(bf16[96,768]{1,0:T(8,128)(2,1)S(1)} %get-tuple-element.148), channel_id=1, source_target_pairs={{0,24},{4,28},{8,16},{12,20},{16,8},{20,12},{24,0},{28,4},{1,25},{... | collective-permute-start | bytes 442376 | tf_op jit(solution)/shard_map/ppermute | solution.py:474
  380.0 23.4 %collective-permute-start.58 = (bf16[96,768]{1,0:T(8,128)(2,1)S(1)}, bf16[96,768]{1,0:T(8,128)(2,1)S(1)}, u32[]{:S(2)}, u32[]{:S(2)}) collective-permute-start(bf16[96,768]{1,0:T(8,128)(2,1)S(1)} %get-tuple-element.149), channel_id=1, source_target_pairs={{0,16},{4,20},{8,24},{12,28},{16,0},{20,4},{24,8},{28,12},{1,17},{... | collective-permute-start | bytes 442376 | tf_op jit(solution)/shard_map/ppermute | solution.py:474
  395.6 21.4 %collective-permute-start.47 = (bf16[4,24,3840]{2,1,0:T(8,128)(2,1)S(1)}, bf16[4,24,3840]{2,1,0:T(8,128)(2,1)S(1)}, u32[]{:S(2)}, u32[]{:S(2)}) collective-permute-start(bf16[4,24,3840]{2,1,0:T(8,128)(2,1)S(1)} %get-tuple-element.112), channel_id=1, source_target_pairs={{0,2},{1,3},{2,0},{3,1},{4,6},{5,7},{6,4},{7,5},{8,10},{9,11},{10,... | collective-permute-start | bytes 2211848 | tf_op jit(solution)/shard_map/ppermute | solution.py:474
  417.0 41.5 %collective-permute-start.63 = (bf16[4,96,768]{2,1,0:T(8,128)(2,1)S(1)}, bf16[4,96,768]{2,1,0:T(8,128)(2,1)S(1)}, u32[]{:S(2)}, u32[]{:S(2)}) collective-permute-start(bf16[4,96,768]{2,1,0:T(8,128)(2,1)S(1)} %get-tuple-element.141), channel_id=1, source_target_pairs={{0,4},{4,0},{8,12},{12,8},{16,20},{20,16},{24,28},{28,24},{1,5},{5... | collective-permute-start | bytes 1769480 | tf_op jit(solution)/shard_map/ppermute | solution.py:474
  423.9 31.4 %collective-permute-start.37 = (bf16[2,4,24,1280]{3,2,1,0:T(8,128)(2,1)S(1)}, bf16[2,4,24,1280]{3,2,1,0:T(8,128)(2,1)S(1)}, u32[]{:S(2)}, u32[]{:S(2)}) collective-permute-start(bf16[2,4,24,1280]{3,2,1,0:T(8,128)(2,1)S(1)} %get-tuple-element.126), channel_id=1, source_target_pairs={{0,4},{4,0},{8,12},{12,8},{16,20},{20,16},{24,28},{28,24},{1,5},{5... | collective-permute-start | bytes 1474568 | tf_op jit(solution)/shard_map/ppermute | solution.py:474
  457.7 31.9 %collective-permute-start.54 = (bf16[4,24,3840]{2,1,0:T(8,128)(2,1)S(1)}, bf16[4,24,3840]{2,1,0:T(8,128)(2,1)S(1)}, u32[]{:S(2)}, u32[]{:S(2)}) collective-permute-start(bf16[4,24,3840]{2,1,0:T(8,128)(2,1)S(1)} %get-tuple-element.132), channel_id=1, source_target_pairs={{0,4},{4,0},{8,12},{12,8},{16,20},{20,16},{24,28},{28,24},{1,5},{5... | collective-permute-start | bytes 2211848 | tf_op jit(solution)/shard_map/ppermute | solution.py:474
  (96 other events, 972.5 us)
Sparse Core Ops, SparseCore 0:
  9.6 33.4 all-gather.6
  45.2 44.1 all-gather.10
  91.0 37.4 all-gather.8
